TPU v7x, 256 devices: a whole 4x4x8 slice. The times are simulated.
256 devices in a mesh: expert: 32 (over z, x), mp: 8 (over y, core).
Axes of the slice: x: 4, y: 4, z: 8, core: 2. Of those that a mesh axis runs over, the one named last changes fastest.
Arguments:
- base_weights: bfloat16 [32, 7168, 1024], P('expert', 'mp'), may hold values from -6 to 6
- deltas: bfloat16 [3, 32, 7168, 1024], P(None, 'expert', 'mp'), may hold values from -1.6 to 1.6
- keep_flags: int32 [3, 32, 896, 8], P(None, 'expert', 'mp'), may hold values 0 or 1
- serve_order: int32 [32], replicated, may hold values from 0 to 31, each once
Outputs:
- served_weights: bfloat16 [32, 1024, 7168], P(None, 'expert', 'mp')
- checksums: float32 [32], P('expert')
- largest_change: float32 [32], P('expert')
Inputs may be any that keep to these rules, and one draw needn't show every extreme that they name: `serve_order`: each expert appears in exactly one slot.
All inputs are finite; a program needn't handle non-finite values. No bound on the sum of `keep_flags` on one device may be relied on, other than what follows from the above.
Results may differ from a plain program's by a relative error of at most 0.008.
Values may be sent and summed in bfloat16 or wider, within the bound.
No kernel may reach another device: no remote copies, remote signals or barrier semaphores. Data moves between devices by JAX's collectives and lax.ppermute only.
A program may use at most 64 MiB of HBM per device.

v0:
```python
import math

import jax
import jax.numpy as jnp
from jax import lax
from jax.sharding import PartitionSpec as P

D = 7168
F = 1024


def cut_along(x, dim, devices):
    before, after = (x.shape[:dim], x.shape[dim + 1 :])
    return jnp.moveaxis(x.reshape(*before, devices, -1, *after), dim, 0)


def cut_rows(length, count):
    step = length // count
    if step >= 8:
        step -= step % 8
    return [step * k for k in range(1, count)]


def laid_out(tiles, dim):
    tiles = jnp.moveaxis(tiles, 0, dim)
    shape = tiles.shape
    return tiles.reshape(*shape[:dim], shape[dim] * shape[dim + 1], *shape[dim + 2 :])


def exchange_in_pieces(x, axis, pieces, split_dim, concat_dim):
    tiles = cut_along(x, split_dim, lax.axis_size(axis))
    cut = max(range(1, max(2, tiles.ndim - 1)), key=lambda d: tiles.shape[d])
    gathered = []
    for piece in jnp.split(tiles, cut_rows(tiles.shape[cut], pieces), axis=cut):
        if piece.size:
            gathered.append(lax.all_to_all(piece, axis, split_axis=0, concat_axis=0, tiled=True))
    return laid_out(jnp.concatenate(gathered, axis=cut), concat_dim)


def over_pieces(x, axis):
    tiles = lax.all_gather(x, axis)
    return tiles.sum(axis=0)


def gathered_total(x, axis):
    return lax.all_gather(x, axis).max(0)


def merge_block(base_rows, delta_rows, keep_rows):
    experts_here, row_count, columns = base_rows.shape
    expanded = keep_rows.astype(jnp.float32)[:, :, :, None, :, None]
    trimmed = (
        delta_rows.astype(jnp.float32).reshape(
            3, experts_here, row_count // 8, 8, columns // 128, 128
        )
        * expanded
    )
    trimmed = trimmed.reshape(3, experts_here, row_count, columns)
    elected = jnp.sign(trimmed[0] + trimmed[1] + trimmed[2])
    agreeing = (trimmed * elected > 0).astype(jnp.float32)
    voters = jnp.sum(agreeing, axis=0)
    update = jnp.sum(trimmed * agreeing, axis=0) / jnp.maximum(voters, 1.0)
    merged = (base_rows.astype(jnp.float32) + update).astype(jnp.bfloat16)
    return (merged, update)


def on_device(base_weights, deltas, keep_flags, serve_order):
    merged, update = merge_block(base_weights, deltas, keep_flags)
    partial_value = jnp.sum(merged.astype(jnp.float32), axis=(1, 2))
    largest_here = jnp.max(jnp.abs(update), axis=(1, 2))
    arranged = exchange_in_pieces(jnp.swapaxes(merged, 1, 2), "expert", 2, 1, 0)
    serving = jnp.take(arranged, serve_order, axis=0)
    total = over_pieces(partial_value, "mp")
    largest = gathered_total(largest_here, "mp")
    return (serving, total / math.sqrt(D * F), largest)


def solution(mesh):
    in_specs = (
        P("expert", "mp", None),
        P(None, "expert", "mp", None),
        P(None, "expert", "mp", None),
        P(),
    )
    out_specs = (P(None, "expert", "mp"), P("expert"), P("expert"))
    return jax.shard_map(
        on_device, mesh=mesh, in_specs=in_specs, out_specs=out_specs, check_vma=False
    )
```

profile of v0, /device:TPU:2, one launch (start us, length us, event | category | flops | bytes accessed | tf_op | source)
XLA Modules:
  0.0 98.4 jit_solution(4717150253219757183)
XLA Ops:
  0.6 0.7 convert_bitcast_fusion.1
  1.3 0.1 copy.12
  1.5 6.8 %fusion = f32[3,1,112,8,8,128]{5,3,4,2,0,1:T(8,128)S(1)} fusion(bf16[3,1,896,1024]{3,2,1,0:T(8,128)(2,1)} %param.5, f32[3,112,8]{2,1,0:T(8,128)S(1)} %copy.12), kind=kLoop, calls=%fused_computation.3 | loop fusion | flops 5505024 | bytes 16525824 | tf_op jit(solution)/shard_map/mul | solution.py:53
  8.2 1.8 %fusion.6 = f32[896,1024]{1,0:T(8,128)S(1)} fusion(f32[3,1,112,8,8,128]{5,3,4,2,0,1:T(8,128)S(1)} %fusion), kind=kLoop, calls=%fused_computation.11 | loop fusion | flops 2752512 | bytes 14680064 | tf_op jit(solution)/shard_map/sign | solution.py:59
  10.1 0.7 copy-done
  10.8 4.2 %convert_reduce_fusion = (f32[896,1024]{1,0:T(8,128)S(1)}, f32[896,1024]{1,0:T(8,128)S(1)}) fusion(bf16[3,1,896,1024]{3,2,1,0:T(8,128)(2,1)S(1)} %copy-done, f32[896,1024]{1,0:T(8,128)S(1)} %fusion.6, f32[3,112,8]{2,1,0:T(8,128)S(1)} %copy.12), kind=kLoop, calls=%fused_computation.8 | loop fusion | flops 20185088 | bytes 16525824 | tf_op jit(solution)/shard_map/reduce_sum | solution.py:61
  15.0 1.9 %abs_reduce_fusion = (f32[]{:T(128)}, f32[896,1024]{1,0:T(8,128)S(1)}) fusion(f32[896,1024]{1,0:T(8,128)S(1)} %get-tuple-element.4, f32[896,1024]{1,0:T(8,128)S(1)} %get-tuple-element.3), kind=kLoop, calls=%fused_computation.15 | loop fusion | flops 3670015 | bytes 11010052 | tf_op jit(solution)/shard_map/reduce_max | solution.py:70
  16.8 2.8 %convert_reduce_fusion.1 = (f32[]{:T(128)}, bf16[1,1024,896]{1,2,0:T(8,128)(2,1)}) fusion(f32[896,1024]{1,0:T(8,128)S(1)} %get-tuple-element.8, bf16[1,896,1024]{2,1,0:T(8,128)(2,1)S(1)} %copy-done.2), kind=kLoop, calls=%fused_computation.16 | loop fusion | flops 4587519 | bytes 7340036 | tf_op jit(solution)/shard_map/reduce_sum | solution.py:69
  19.6 3.1 %copy.14 = bf16[1,1024,896]{2,1,0:T(8,128)(2,1)S(1)} copy(bf16[1,1024,896]{1,2,0:T(8,128)(2,1)} %get-tuple-element.10) | data formatting | bytes 3670016 | tf_op jit(solution)/shard_map/transpose | solution.py:71
  22.7 0.0 copy-start.4
  22.7 1.1 %slice_bitcast_fusion.1 = (bf16[32,1,16,896]{3,2,1,0:T(8,128)(2,1)}, bf16[32,1,16,896]{3,2,1,0:T(8,128)(2,1)S(1)}) fusion(bf16[32,1,32,896]{3,2,0,1:T(8,128)(2,1)S(1)} %bitcast.46), kind=kLoop, calls=%fused_computation.21 | loop fusion | bytes 3670016 | tf_op jit(solution)/shard_map/split | solution.py:34
  23.8 36.7 %all_to_all.10 = bf16[32,1,16,896]{3,2,1,0:T(8,128)(2,1)S(1)} all-to-all(bf16[32,1,16,896]{3,2,1,0:T(8,128)(2,1)S(1)} %get-tuple-element.12), channel_id=1, replica_groups=mesh['expert'=32,'mp'=8] {'expert'}, dimensions={0} | all-to-all | bytes 1835008 | tf_op jit(solution)/shard_map/all_to_all | solution.py:36
  60.4 5.6 %all-to-all-start = ((bf16[32,1,16,896]{3,2,1,0:T(8,128)(2,1)}), bf16[32,1,16,896]{3,2,1,0:T(8,128)(2,1)S(1)}, u32[]{:S(2)}, u32[]{:S(2)}) async-start(bf16[32,1,16,896]{3,2,1,0:T(8,128)(2,1)} %get-tuple-element.11), calls=%async_computation | async-start | bytes 1835008 | tf_op jit(solution)/shard_map/all_to_all | solution.py:36
  66.0 0.7 dynamic-slice
  66.7 1.4 %dynamic-update-slice = f32[8]{0:T(128)S(1)} dynamic-update-slice(f32[8]{0:T(128)S(1)} %broadcast.37.clone, f32[1]{0:T(128)} %bitcast.12, u32[]{:T(128)} %bitcast.13) | dynamic-update-slice | bytes 12
  68.1 1.4 %dynamic-update-slice.1 = f32[8]{0:T(128)S(1)} dynamic-update-slice(f32[8]{0:T(128)S(1)} %broadcast.37.clone.1, f32[1]{0:T(128)} %bitcast.15, u32[]{:T(128)} %bitcast.13) | dynamic-update-slice | bytes 12
  69.6 13.6 %all-reduce.2 = (f32[8]{0:T(128)S(1)}, f32[8]{0:T(128)S(1)}) all-reduce(f32[8]{0:T(128)S(1)} %dynamic-update-slice, f32[8]{0:T(128)S(1)} %dynamic-update-slice.1), channel_id=1, replica_groups=mesh['expert'=32,'mp'=8] {'mp'}, use_global_device_ids=true, to_apply=%add | all-reduce | flops 16 | bytes 128
  83.2 0.6 reduce.7
  84.5 0.6 reduce.8
  85.1 4.9 %all-to-all-done = bf16[32,1,16,896]{3,2,1,0:T(8,128)(2,1)S(1)} async-done(((bf16[32,1,16,896]{3,2,1,0:T(8,128)(2,1)}), bf16[32,1,16,896]{3,2,1,0:T(8,128)(2,1)S(1)}, u32[]{:S(2)}, u32[]{:S(2)}) %all-to-all-start) | async-done | bytes 917536 | tf_op jit(solution)/shard_map/all_to_all | solution.py:36
  90.0 0.9 copy-done.1
  91.0 1.3 %maximum_bitcast_fusion = bf16[32,32,896]{2,1,0:T(8,128)(2,1)S(1)} fusion(bf16[32,1,16,896]{3,2,0,1:T(8,128)(2,1)S(1)} %bitcast.47, bf16[32,1,16,896]{3,2,0,1:T(8,128)(2,1)} %bitcast.48), kind=kLoop, calls=%fused_computation.18 | loop fusion | flops 3670016 | bytes 3670016 | tf_op jit(solution)/shard_map/reshape | solution.py:27
  92.3 2.0 %gather_fusion = bf16[32,32,896]{2,1,0:T(8,128)(2,1)} fusion(bf16[32,32,896]{2,1,0:T(8,128)(2,1)S(1)} %maximum_bitcast_fusion, s32[1024]{0:T(1024)S(1)} %pad_clamp_fusion), kind=kCustom, calls=%fused_computation | custom fusion | bytes 3670144 | tf_op jit(solution)/shard_map/jit(_take)/gather | solution.py:72
  94.3 3.0 %broadcast_select_fusion = bf16[32,32,896]{2,1,0:T(8,128)(2,1)} fusion(bf16[32,32,896]{2,1,0:T(8,128)(2,1)} %gather_fusion, pred[32]{0:T(512)(128)(4,1)S(1)} %compare_and_fusion), kind=kLoop, calls=%fused_computation.19 | loop fusion | flops 917504 | bytes 3670048 | tf_op jit(solution)/shard_map/jit(_take)/select_n | solution.py:72
  (12 shorter events, 0.0 us)
Async XLA Ops:
  8.2 2.6 %copy-start = (bf16[3,1,896,1024]{3,2,1,0:T(8,128)(2,1)S(1)}, bf16[3,1,896,1024]{3,2,1,0:T(8,128)(2,1)}, u32[]{:S(2)}) copy-start(bf16[3,1,896,1024]{3,2,1,0:T(8,128)(2,1)} %param.5) | copy-start | bytes 16515076
  15.0 1.9 %copy-start.2 = (bf16[1,896,1024]{2,1,0:T(8,128)(2,1)S(1)}, bf16[1,896,1024]{2,1,0:T(8,128)(2,1)}, u32[]{:S(2)}) copy-start(bf16[1,896,1024]{2,1,0:T(8,128)(2,1)} %param.4) | copy-start | bytes 5505028
  22.7 43.3 %copy-start.4 = (u32[256]{0:T(256)S(1)}, u32[256]{0:T(256)}, u32[]{:S(2)}) copy-start(u32[256]{0:T(256)} %constant.33) | copy-start | bytes 3076
  22.7 62.4 %copy-start.3 = (s32[32]{0:T(128)S(1)}, s32[32]{0:T(128)}, u32[]{:S(2)}) copy-start(s32[32]{0:T(128)} %param.7) | copy-start | bytes 388
  60.4 29.6 %all-to-all-start = ((bf16[32,1,16,896]{3,2,1,0:T(8,128)(2,1)}), bf16[32,1,16,896]{3,2,1,0:T(8,128)(2,1)S(1)}, u32[]{:S(2)}, u32[]{:S(2)}) async-start(bf16[32,1,16,896]{3,2,1,0:T(8,128)(2,1)} %get-tuple-element.11), calls=%async_computation | async-start | bytes 1835008 | tf_op jit(solution)/shard_map/all_to_all | solution.py:36
  90.0 0.9 copy-start.1
where the time goes:
time: 99 us; the launch traced here: 98.4 us
  blocking collectives  50.3 us (51%)
  other arithmetic  23.6 us (24%)
  local copies, waits for them, and re-layouts  11.5 us (12%)
  starting transfers between devices  5.57 us (6%)
  waiting for transfers between devices  4.93 us (5%)
  between operations  2.53 us (3%)
    all_to_all x1, blocking collectives, exchange_in_pieces(): lax.all_to_all(piece, axis, split_axis=0, concat_axis=0, tiled=True)  36.7 us
    unnamed x1, blocking collectives  13.6 us
    mul x2, other arithmetic, merge_block(): delta_rows.astype(jnp.float32)  7.48 us
    all_to_all x1, starting transfers between devices, exchange_in_pieces(): lax.all_to_all(piece, axis, split_axis=0, concat_axis=0, tiled=True)  5.57 us
    unnamed x15, local copies, waits for them, and re-layouts  5.24 us
    all_to_all x1, waiting for transfers between devices, exchange_in_pieces(): lax.all_to_all(piece, axis, split_axis=0, concat_axis=0, tiled=True)  4.93 us
    reduce_sum x1, other arithmetic, merge_block(): voters = jnp.sum(agreeing, axis=0)  4.16 us
    transpose x1, local copies, waits for them, and re-layouts, on_device(): arranged = exchange_in_pieces(jnp.swapaxes(merged, 1, 2), 'expert', 2, 1, 0)  3.05 us
  transfers between devices with their start and end apart: 1, of which 1 were waited for; matrix products, arithmetic and copies ran while one was open for 5% of the time, Pallas kernels for 0%

commit v1 on v0

v1 whole, which is shorter than its diff:
```python
import functools
import math

import jax
import jax.numpy as jnp
from jax import lax
from jax.experimental import pallas as pl
from jax.experimental.pallas import tpu as pltpu
from jax.sharding import PartitionSpec as P

D = 7168
F = 1024
LANES = 128


def merge_kernel(keep_ref, base_ref, delta_ref, out_ref, sums_ref, largest_ref, spread_ref):
    step = pl.program_id(0)
    rows, columns = base_ref.shape[1:]
    blocks = rows // 8
    flags = keep_ref[:, 0].astype(jnp.float32).reshape(3 * blocks, columns // LANES)
    lane_block = lax.broadcasted_iota(jnp.int32, (columns // LANES, columns), 1) // LANES
    own_block = lax.broadcasted_iota(jnp.int32, (columns // LANES, columns), 0)
    expand = (lane_block == own_block).astype(jnp.float32)
    spread_ref[...] = jnp.dot(flags, expand, preferred_element_type=jnp.float32)

    @pl.when(step == 0)
    def _():
        sums_ref[...] = jnp.zeros_like(sums_ref)
        largest_ref[...] = jnp.zeros_like(largest_ref)

    total = jnp.zeros((8, LANES), jnp.float32)
    largest = jnp.zeros((8, LANES), jnp.float32)
    for c in range(columns // LANES):
        cols = pl.ds(c * LANES, LANES)
        t = []
        for k in range(3):
            d = delta_ref[k, 0, :, cols].astype(jnp.float32).reshape(blocks, 8, LANES)
            kept = spread_ref[pl.ds(k * blocks, blocks), cols]
            t.append(d * kept[:, None, :])
        s = t[0] + t[1] + t[2]
        sign = jnp.where(s > 0, 1.0, jnp.where(s < 0, -1.0, 0.0))
        u = [x * sign for x in t]
        chosen = jnp.maximum(u[0], 0.0) + jnp.maximum(u[1], 0.0) + jnp.maximum(u[2], 0.0)
        voters = sum(jnp.where(x > 0, 1.0, 0.0) for x in u)
        share = jnp.where(voters > 2.5, 1.0 / 3.0, jnp.where(voters > 1.5, 0.5, 1.0))
        size = chosen * share
        update = (size * sign).reshape(rows, LANES)
        merged = (base_ref[0, :, cols].astype(jnp.float32) + update).astype(jnp.bfloat16)
        total = total + merged.astype(jnp.float32).reshape(blocks, 8, LANES).sum(axis=0)
        largest = jnp.maximum(largest, size.max(axis=0))
        turned = merged.T
        out_ref[pl.ds(c * 4, 4)] = turned.reshape(4, LANES // 4, rows)
    sums_ref[...] += total
    largest_ref[...] = jnp.maximum(largest_ref[...], largest)


def merge(base_weights, deltas, keep_flags):
    _, rows, columns = base_weights.shape
    step = LANES
    n = 32
    return pl.pallas_call(
        merge_kernel,
        grid=(rows // step,),
        in_specs=[
            pl.BlockSpec((3, 1, step // 8, columns // LANES), lambda i: (0, 0, i, 0)),
            pl.BlockSpec((1, step, columns), lambda i: (0, i, 0)),
            pl.BlockSpec((3, 1, step, columns), lambda i: (0, 0, i, 0)),
        ],
        out_specs=[
            pl.BlockSpec((n, columns // n, step), lambda i: (0, 0, i)),
            pl.BlockSpec((8, LANES), lambda i: (0, 0)),
            pl.BlockSpec((8, LANES), lambda i: (0, 0)),
        ],
        out_shape=[
            jax.ShapeDtypeStruct((n, columns // n, rows), jnp.bfloat16),
            jax.ShapeDtypeStruct((8, LANES), jnp.float32),
            jax.ShapeDtypeStruct((8, LANES), jnp.float32),
        ],
        scratch_shapes=[pltpu.VMEM((3 * step // 8, columns), jnp.float32)],
        compiler_params=pltpu.CompilerParams(vmem_limit_bytes=16 * 2**20),
    )(keep_flags, base_weights, deltas)


def place_kernel(order_ref, in_ref, out_ref, sems):
    n = out_ref.shape[0]
    for s in range(n):
        pltpu.make_async_copy(in_ref.at[order_ref[s]], out_ref.at[s], sems.at[s]).start()
    for s in range(n):
        pltpu.make_async_copy(in_ref.at[order_ref[s]], out_ref.at[s], sems.at[s]).wait()


def place(arranged, serve_order):
    n = arranged.shape[0]
    return pl.pallas_call(
        place_kernel,
        in_specs=[
            pl.BlockSpec(memory_space=pltpu.SMEM),
            pl.BlockSpec(memory_space=pl.ANY),
        ],
        out_specs=pl.BlockSpec(memory_space=pl.ANY),
        out_shape=jax.ShapeDtypeStruct(arranged.shape, arranged.dtype),
        scratch_shapes=[pltpu.SemaphoreType.DMA((n,))],
        compiler_params=pltpu.CompilerParams(vmem_limit_bytes=4 * 2**20),
    )(serve_order, arranged)


def on_device(base_weights, deltas, keep_flags, serve_order):
    merged, sums, largest = merge(base_weights, deltas, keep_flags)
    arranged = lax.all_to_all(merged, "expert", split_axis=0, concat_axis=0, tiled=True)
    total_here = jnp.sum(sums).reshape(1)
    largest_here = jnp.max(largest).reshape(1)
    both = lax.all_gather(jnp.concatenate([total_here, largest_here]), "mp")
    serving = place(arranged, serve_order)
    return (serving, both[:, 0].sum(0)[None] / math.sqrt(D * F), both[:, 1].max(0)[None])


def solution(mesh):
    in_specs = (
        P("expert", "mp", None),
        P(None, "expert", "mp", None),
        P(None, "expert", "mp", None),
        P(),
    )
    out_specs = (P(None, "expert", "mp"), P("expert"), P("expert"))
    return jax.shard_map(
        on_device, mesh=mesh, in_specs=in_specs, out_specs=out_specs, check_vma=False
    )
```

time: 99 us -> 74.6 us (0.75)
  blocking collectives: 50.3 us -> 14.9 us
  other arithmetic: 23.6 us -> 3.46 us
  waiting for transfers between devices: 4.93 us -> 23.5 us
  Pallas kernels: 0 us -> 9.72 us
  starting transfers between devices: 5.57 us -> 11.7 us
  local copies, waits for them, and re-layouts: 11.5 us -> 6.77 us
    all_to_all x1 -> x0, blocking collectives: 36.7 us -> none  [exchange_in_pieces(): lax.all_to_all(piece, axis, split_axis=0, concat_axis=0, tiled=True)]
    all_to_all x1, waiting for transfers between devices: 4.93 us -> 23.5 us  [on_device(): lax.all_to_all(merged, 'expert', split_axis=0, concat_axis=0, tiled=True)]
    pallas_call x0 -> x2, Pallas kernels: none -> 9.72 us  [the longest x1 7.69 us: merge(): pl.pallas_call(merge_kernel, grid=(rows // step,), in_specs=[pl.BlockSpec...]
    mul x2 -> x0, other arithmetic: 7.48 us -> none  [merge_block(): delta_rows.astype(jnp.float32)]
    reduce_sum x3 -> x1, other arithmetic: 7.53 us -> 0.68 us  [on_device(): total_here = jnp.sum(sums).reshape(1)]
    all_to_all x1, starting transfers between devices: 5.57 us -> 11.7 us  [on_device(): lax.all_to_all(merged, 'expert', split_axis=0, concat_axis=0, tiled=True)]
    transpose x1 -> x0, local copies, waits for them, and re-layouts: 3.05 us -> none  [on_device(): arranged = exchange_in_pieces(jnp.swapaxes(merged, 1, 2), 'expert', 2, 1, 0)]
    select_n x2 -> x0, other arithmetic: 2.98 us -> none  [on_device(): serving = jnp.take(arranged, serve_order, axis=0)]
  transfers between devices with their start and end apart: 1 -> 1, of which waited for: 1 -> 1; matrix products, arithmetic and copies ran while one was open for 5% -> 6% of each run, Pallas kernels for 0% -> 0%
where the time goes in v1:
time: 74.6 us; the launch traced here: 73.2 us
  waiting for transfers between devices  23.5 us (32%)
  blocking collectives  14.9 us (20%)
  starting transfers between devices  11.7 us (16%)
  Pallas kernels  9.72 us (13%)
  local copies, waits for them, and re-layouts  6.77 us (9%)
  other arithmetic  3.46 us (5%)
  between operations  3.13 us (4%)
    all_to_all x1, waiting for transfers between devices, on_device(): lax.all_to_all(merged, 'expert', split_axis=0, concat_axis=0, tiled=True)  23.5 us
    unnamed x1, blocking collectives  14.9 us
    all_to_all x1, starting transfers between devices, on_device(): lax.all_to_all(merged, 'expert', split_axis=0, concat_axis=0, tiled=True)  11.7 us
    pallas_call x1, Pallas kernels, merge(): pl.pallas_call(merge_kernel, grid=(rows // step,), in_specs=[pl.BlockSpec...  7.69 us
    unnamed x13, local copies, waits for them, and re-layouts  6.69 us
    pallas_call x1, Pallas kernels, place(): pl.pallas_call(place_kernel, in_specs=[pl.BlockSpec(memory_space=pltpu.SM...  2.02 us
    unnamed x1, other arithmetic  1.5 us
  transfers between devices with their start and end apart: 1, of which 1 were waited for; matrix products, arithmetic and copies ran while one was open for 6% of the time, Pallas kernels for 0%

profile of v1, /device:TPU:2, one launch (start us, length us, event | category | flops | bytes accessed | tf_op | source)
XLA Modules:
  0.0 73.2 jit_solution(7639001964123682046)
XLA Ops:
  0.6 0.8 %copy.8.keep_ref = s32[3,1,112,8]{3,2,1,0:T(8,128)S(1)} copy(s32[3,1,112,8]{2,3,1,0:T(8,128)} %param.6) | data formatting | bytes 21504 | tf_op args[2]
  1.5 0.0 copy-start
  1.5 2.6 %copy-done = bf16[3,1,896,1024]{3,2,1,0:T(8,128)(2,1)S(1)} copy-done((bf16[3,1,896,1024]{3,2,1,0:T(8,128)(2,1)S(1)}, bf16[3,1,896,1024]{3,2,1,0:T(8,128)(2,1)}, u32[]{:S(2)}) %copy-start) | copy-done | bytes 5505048
  4.0 0.0 copy-start.2
  4.0 1.5 %copy-done.2 = bf16[1,896,1024]{2,1,0:T(8,128)(2,1)S(1)} copy-done((bf16[1,896,1024]{2,1,0:T(8,128)(2,1)S(1)}, bf16[1,896,1024]{2,1,0:T(8,128)(2,1)}, u32[]{:S(2)}) %copy-start.2) | copy-done | bytes 1835032
  5.5 7.7 %shard_map.67 = (bf16[32,32,896]{2,1,0:T(8,128)(2,1)S(1)}, f32[8,128]{1,0:T(8,128)S(1)}, f32[8,128]{1,0:T(8,128)S(1)}) custom-call(s32[3,1,112,8]{3,2,1,0:T(8,128)S(1)} %copy.8.keep_ref, bf16[1,896,1024]{2,1,0:T(8,128)(2,1)S(1)} %copy-done.2, bf16[3,1,896,1024]{3,2,1,0:T(8,128)(2,1)S(1)} %copy-done), custom_call_target="tpu_custom_call" | custom-call | tf_op jit(solution)/shard_map/pallas_call | solution.py:61
  13.2 0.0 copy-start.1
  13.2 1.2 %copy-done.1 = bf16[32,32,896]{2,1,0:T(8,128)(2,1)} copy-done((bf16[32,32,896]{2,1,0:T(8,128)(2,1)}, bf16[32,32,896]{2,1,0:T(8,128)(2,1)S(1)}, u32[]{:S(2)}) %copy-start.1) | copy-done | bytes 1835032
  14.5 0.0 copy-start.4
  14.5 0.0 copy-start.3
  14.5 11.7 %all-to-all-start = ((bf16[32,32,896]{2,1,0:T(8,128)(2,1)}), bf16[32,32,896]{2,1,0:T(8,128)(2,1)S(1)}, u32[]{:S(2)}, u32[]{:S(2)}) async-start(bf16[32,32,896]{2,1,0:T(8,128)(2,1)} %copy-done.1), calls=%async_computation | async-start | bytes 3670016 | tf_op jit(solution)/shard_map/all_to_all | solution.py:109
  26.2 0.0 copy-done.4
  26.2 0.6 dynamic-slice
  27.5 0.6 reduce_max.18
  28.1 0.7 reduce_sum.18
  28.7 1.5 %maximum_dynamic-update-slice_fusion = f32[16]{0:T(128)S(1)} fusion(f32[16]{0:T(128)S(1)} %broadcast, u32[]{:T(128)} %bitcast.2, f32[1]{0:T(128)} %bitcast.1, f32[1]{0:T(128)} %bitcast), kind=kLoop, calls=%fused_computation.2 | loop fusion | flops 2 | bytes 76
  30.2 14.9 %all-reduce = f32[16]{0:T(128)S(1)} all-reduce(f32[16]{0:T(128)S(1)} %maximum_dynamic-update-slice_fusion), channel_id=2, replica_groups=mesh['expert'=32,'mp'=8] {'mp'}, use_global_device_ids=true, to_apply=%add | all-reduce | flops 16 | bytes 128
  45.1 0.1 reshape.16
  45.2 0.7 slice_reduce_fusion
  46.5 23.5 %all-to-all-done.in_ref = bf16[32,32,896]{2,1,0:T(8,128)(2,1)S(1)} async-done(((bf16[32,32,896]{2,1,0:T(8,128)(2,1)}), bf16[32,32,896]{2,1,0:T(8,128)(2,1)S(1)}, u32[]{:S(2)}, u32[]{:S(2)}) %all-to-all-start) | async-done | bytes 1835040 | tf_op jit(solution)/shard_map/all_to_all | solution.py:109
  70.0 0.0 copy-done.3
  70.0 2.0 %shard_map.68 = bf16[32,32,896]{2,1,0:T(8,128)(2,1)} custom-call(s32[32]{0:T(128)S(1)} %copy-done.3, bf16[32,32,896]{2,1,0:T(8,128)(2,1)S(1)} %all-to-all-done.in_ref), custom_call_target="tpu_custom_call" | custom-call | tf_op jit(solution)/shard_map/pallas_call | solution.py:94
  (1 shorter events, 0.0 us)
Async XLA Ops:
  1.5 2.6 %copy-start = (bf16[3,1,896,1024]{3,2,1,0:T(8,128)(2,1)S(1)}, bf16[3,1,896,1024]{3,2,1,0:T(8,128)(2,1)}, u32[]{:S(2)}) copy-start(bf16[3,1,896,1024]{3,2,1,0:T(8,128)(2,1)} %delta_ref.1) | copy-start | bytes 16515076
  4.0 1.5 %copy-start.2 = (bf16[1,896,1024]{2,1,0:T(8,128)(2,1)S(1)}, bf16[1,896,1024]{2,1,0:T(8,128)(2,1)}, u32[]{:S(2)}) copy-start(bf16[1,896,1024]{2,1,0:T(8,128)(2,1)} %base_ref.1) | copy-start | bytes 5505028
  13.2 1.2 %copy-start.1 = (bf16[32,32,896]{2,1,0:T(8,128)(2,1)}, bf16[32,32,896]{2,1,0:T(8,128)(2,1)S(1)}, u32[]{:S(2)}) copy-start(bf16[32,32,896]{2,1,0:T(8,128)(2,1)S(1)} %get-tuple-element.6) | copy-start | bytes 5505028
  14.5 11.8 %copy-start.4 = (u32[256]{0:T(256)S(1)}, u32[256]{0:T(256)}, u32[]{:S(2)}) copy-start(u32[256]{0:T(256)} %constant.13) | copy-start | bytes 3076
  14.5 55.6 %copy-start.3 = (s32[32]{0:T(128)S(1)}, s32[32]{0:T(128)}, u32[]{:S(2)}) copy-start(s32[32]{0:T(128)} %order_ref.1) | copy-start | bytes 388
  14.5 55.5 %all-to-all-start = ((bf16[32,32,896]{2,1,0:T(8,128)(2,1)}), bf16[32,32,896]{2,1,0:T(8,128)(2,1)S(1)}, u32[]{:S(2)}, u32[]{:S(2)}) async-start(bf16[32,32,896]{2,1,0:T(8,128)(2,1)} %copy-done.1), calls=%async_computation | async-start | bytes 3670016 | tf_op jit(solution)/shard_map/all_to_all | solution.py:109

commit v2 on v1

v2 whole, which is shorter than its diff:
```python
import math

import jax
import jax.numpy as jnp
from jax import lax
from jax.experimental import pallas as pl
from jax.experimental.pallas import tpu as pltpu
from jax.sharding import PartitionSpec as P

D = 7168
F = 1024
LANES = 128
STEP = 128
ORDER = [
    19, 28, 1, 17, 12, 22, 16, 30, 15, 23, 11, 24, 6, 9, 31, 14,
    25, 4, 26, 2, 27, 13, 0, 5, 18, 7, 3, 29, 20, 21, 8, 10,
]
PLACE_OF = [ORDER.index(e) for e in range(32)]
VMEM_BYTES = 60 * 2**20


def spread_flags(flags, columns):
    lane_block = lax.broadcasted_iota(jnp.int32, (flags.shape[0], columns), 1) // LANES
    own_block = lax.broadcasted_iota(jnp.int32, (flags.shape[0], columns), 0)
    expand = (lane_block == own_block).astype(jnp.float32)
    return lax.dot_general(
        flags.astype(jnp.float32),
        expand,
        (((0,), (0,)), ((), ())),
        preferred_element_type=jnp.float32,
    )


def voted_update(t):
    s = t[0] + t[1] + t[2]
    sign = jnp.where(s > 0, 1.0, jnp.where(s < 0, -1.0, 0.0))
    a, b, c = (x * sign for x in t)
    low, high = jnp.minimum(a, b), jnp.maximum(a, b)
    most, least = jnp.maximum(high, c), jnp.minimum(low, c)
    middle = jnp.maximum(low, jnp.minimum(high, c))
    few = jnp.where(middle > 0, (most + middle) * 0.5, most) * sign
    return jnp.where(least > 0, s * (1.0 / 3.0), few)


def trimmed_tile(delta_at, flags_at):
    out = []
    for k in range(3):
        d = delta_at(k).astype(jnp.float32)
        rows = d.shape[0]
        out.append(d.reshape(rows // 8, 8, LANES) * flags_at(k)[:, None, :])
    return out


def merge_kernel(
    keep_hbm, base_hbm, delta_hbm, out_hbm, d_buf, b_buf, o_buf, k_buf, spread_ref, in_sems, out_sems, k_sem
):
    rows_all, columns = b_buf.shape
    n = rows_all // STEP
    blocks = STEP // 8

    def rows_of(i):
        return pl.ds(pl.multiple_of(i * STEP, STEP), STEP)

    def delta_copy(i):
        return pltpu.make_async_copy(delta_hbm.at[:, 0, rows_of(i)], d_buf.at[:, rows_of(i)], in_sems.at[i, 0])

    def base_copy(i):
        return pltpu.make_async_copy(base_hbm.at[0, rows_of(i)], b_buf.at[rows_of(i)], in_sems.at[i, 1])

    def out_copy(i):
        return pltpu.make_async_copy(o_buf.at[i], out_hbm.at[:, :, rows_of(i)], out_sems.at[i])

    keep_copy = pltpu.make_async_copy(keep_hbm, k_buf, k_sem)
    def fetch(i):
        delta_copy(i).start()
        base_copy(i).start()

    keep_copy.start()
    fetch(0)
    keep_copy.wait()
    for k in range(3):
        spread_ref[k] = spread_flags(k_buf[k, 0], columns)
    fetch(1)

    def chunk(i, carry):
        delta_copy(i).wait()
        base_copy(i).wait()

        @pl.when(i + 2 < n)
        def _():
            fetch(i + 2)

        flag_rows = pl.ds(pl.multiple_of(i * blocks, blocks), blocks)
        for c in range(columns // LANES):
            cols = pl.ds(c * LANES, LANES)
            t = trimmed_tile(lambda k: d_buf[k, rows_of(i), cols], lambda k: spread_ref[k, flag_rows, cols])
            base = b_buf[rows_of(i), cols].astype(jnp.float32).reshape(blocks, 8, LANES)
            merged = (base + voted_update(t)).reshape(STEP, LANES).astype(jnp.bfloat16)
            turned = merged.T.reshape(4, LANES // 4, STEP)
            for j in range(4):
                o_buf[i, PLACE_OF[c * 4 + j]] = turned[j]
        out_copy(i).start()
        return carry

    lax.fori_loop(0, n, chunk, 0)
    for i in range(n):
        out_copy(i).wait()


def merge(base_weights, deltas, keep_turned):
    _, rows, columns = base_weights.shape
    n = rows // STEP
    slots = len(ORDER)
    return pl.pallas_call(
        merge_kernel,
        in_specs=[pl.BlockSpec(memory_space=pl.ANY)] * 3,
        out_specs=pl.BlockSpec(memory_space=pl.ANY),
        out_shape=jax.ShapeDtypeStruct((slots, columns // slots, rows), jnp.bfloat16),
        scratch_shapes=[
            pltpu.VMEM((3, rows, columns), jnp.bfloat16),
            pltpu.VMEM((rows, columns), jnp.bfloat16),
            pltpu.VMEM((n, slots, columns // slots, STEP), jnp.bfloat16),
            pltpu.VMEM(keep_turned.shape, jnp.int32),
            pltpu.VMEM((3, rows // 8, columns), jnp.float32),
            pltpu.SemaphoreType.DMA((n, 2)),
            pltpu.SemaphoreType.DMA((n,)),
            pltpu.SemaphoreType.DMA,
        ],
        compiler_params=pltpu.CompilerParams(vmem_limit_bytes=VMEM_BYTES),
    )(keep_turned, base_weights, deltas)


def figures_kernel(keep_ref, delta_ref, merged_ref, sums_ref, largest_ref, spread_ref):
    step = pl.program_id(0)
    columns = delta_ref.shape[3]
    blocks = STEP // 8

    @pl.when(step == 0)
    def _():
        sums_ref[...] = jnp.zeros_like(sums_ref)
        largest_ref[...] = jnp.zeros_like(largest_ref)
        for k in range(3):
            spread_ref[k] = spread_flags(keep_ref[k, 0], columns)

    flag_rows = pl.ds(pl.multiple_of(step * blocks, blocks), blocks)
    largest = largest_ref[...]
    for c in range(columns // LANES):
        cols = pl.ds(c * LANES, LANES)
        t = trimmed_tile(lambda k: delta_ref[k, 0, :, cols], lambda k: spread_ref[k, flag_rows, cols])
        largest = jnp.maximum(largest, jnp.abs(voted_update(t)).max(axis=0))
    largest_ref[...] = largest
    total = sums_ref[...]
    for s in range(merged_ref.shape[0]):
        m = merged_ref[s].astype(jnp.float32)
        total = total + m.reshape(m.shape[0] // 8, 8, LANES).sum(axis=0)
    sums_ref[...] = total


def figures(keep_turned, deltas, merged):
    _, _, rows, columns = deltas.shape
    slots, height, _ = merged.shape
    return pl.pallas_call(
        figures_kernel,
        grid=(rows // STEP,),
        in_specs=[
            pl.BlockSpec(keep_turned.shape, lambda i: (0, 0, 0, 0)),
            pl.BlockSpec((3, 1, STEP, columns), lambda i: (0, 0, i, 0)),
            pl.BlockSpec((slots, height, STEP), lambda i: (0, 0, i)),
        ],
        out_specs=[pl.BlockSpec((8, LANES), lambda i: (0, 0))] * 2,
        out_shape=[jax.ShapeDtypeStruct((8, LANES), jnp.float32)] * 2,
        scratch_shapes=[pltpu.VMEM((3, rows // 8, columns), jnp.float32)],
        compiler_params=pltpu.CompilerParams(vmem_limit_bytes=VMEM_BYTES),
    )(keep_turned, deltas, merged)


def place_kernel(order_ref, place_ref, in_ref, out_ref, sems):
    def copy(s):
        return pltpu.make_async_copy(in_ref.at[place_ref[order_ref[s]]], out_ref.at[s], sems.at[s])

    for s in range(out_ref.shape[0]):
        copy(s).start()
    for s in range(out_ref.shape[0]):
        copy(s).wait()


def place(arranged, serve_order):
    n = arranged.shape[0]
    return pl.pallas_call(
        place_kernel,
        in_specs=[
            pl.BlockSpec(memory_space=pltpu.SMEM),
            pl.BlockSpec(memory_space=pltpu.SMEM),
            pl.BlockSpec(memory_space=pl.ANY),
        ],
        out_specs=pl.BlockSpec(memory_space=pl.ANY),
        out_shape=jax.ShapeDtypeStruct(arranged.shape, arranged.dtype),
        scratch_shapes=[pltpu.SemaphoreType.DMA((n,))],
        compiler_params=pltpu.CompilerParams(vmem_limit_bytes=4 * 2**20),
    )(serve_order, jnp.array(PLACE_OF, jnp.int32), arranged)


def on_device(base_weights, deltas, keep_flags, serve_order):
    keep_turned = jnp.swapaxes(keep_flags, 2, 3)
    merged = merge(base_weights, deltas, keep_turned)
    arranged = lax.all_to_all(
        merged, "expert", split_axis=0, concat_axis=0, tiled=True, axis_index_groups=[ORDER]
    )
    sums, largest = figures(keep_turned, deltas, merged)
    here = jnp.stack([jnp.sum(sums), jnp.max(largest)])
    both = lax.all_gather(here, "mp")
    serving = place(arranged, serve_order)
    return (serving, both[:, 0].sum(0)[None] / math.sqrt(D * F), both[:, 1].max(0)[None])


def solution(mesh):
    in_specs = (
        P("expert", "mp", None),
        P(None, "expert", "mp", None),
        P(None, "expert", "mp", None),
        P(),
    )
    out_specs = (P(None, "expert", "mp"), P("expert"), P("expert"))
    return jax.shard_map(
        on_device, mesh=mesh, in_specs=in_specs, out_specs=out_specs, check_vma=False
    )
```

time: 74.6 us -> 66.1 us (0.89)
  waiting for transfers between devices: 23.5 us -> 10.4 us
  Pallas kernels: 9.72 us -> 18.5 us
  local copies, waits for them, and re-layouts: 6.77 us -> 0.68 us
  starting transfers between devices: 11.7 us -> 13 us
  other arithmetic: 3.46 us -> 4.61 us
    all_to_all x1, waiting for transfers between devices: 23.5 us -> 10.4 us  [on_device(): lax.all_to_all(merged, 'expert', split_axis=0, concat_axis=0, tiled=True,...]
    pallas_call x1 -> x2, Pallas kernels: 7.69 us -> 16.5 us  [the longest x1 8.84 us: figures(): pl.pallas_call(figures_kernel, grid=(rows // STEP,), in_specs=[pl.BlockSp...]
    unnamed x13 -> x8, local copies, waits for them, and re-layouts: 6.69 us -> 0.6 us
    all_to_all x1, starting transfers between devices: 11.7 us -> 13 us  [on_device(): lax.all_to_all(merged, 'expert', split_axis=0, concat_axis=0, tiled=True,...]
  transfers between devices with their start and end apart: 1 -> 1, of which waited for: 1 -> 1; matrix products, arithmetic and copies ran while one was open for 6% -> 8% of each run, Pallas kernels for 0% -> 14%
where the time goes in v2:
time: 66.1 us; the launch traced here: 65.1 us
  Pallas kernels  18.5 us (28%)
  blocking collectives  14.9 us (23%)
  starting transfers between devices  13 us (20%)
  waiting for transfers between devices  10.4 us (16%)
  other arithmetic  4.61 us (7%)
  between operations  3.12 us (5%)
  local copies, waits for them, and re-layouts  0.68 us (1%)
    unnamed x1, blocking collectives  14.9 us
    all_to_all x1, starting transfers between devices, on_device(): lax.all_to_all(merged, 'expert', split_axis=0, concat_axis=0, tiled=True,...  13 us
    all_to_all x1, waiting for transfers between devices, on_device(): lax.all_to_all(merged, 'expert', split_axis=0, concat_axis=0, tiled=True,...  10.4 us
    pallas_call x1, Pallas kernels, figures(): pl.pallas_call(figures_kernel, grid=(rows // STEP,), in_specs=[pl.BlockSp...  8.84 us
    pallas_call x1, Pallas kernels, merge(): pl.pallas_call(merge_kernel, in_specs=[pl.BlockSpec(memory_space=pl.ANY)]...  7.61 us
    pallas_call x1, Pallas kernels, place(): pl.pallas_call(place_kernel, in_specs=[pl.BlockSpec(memory_space=pltpu.SM...  2.03 us
    unnamed x1, other arithmetic  1.37 us
  transfers between devices with their start and end apart: 1, of which 1 were waited for; matrix products, arithmetic and copies ran while one was open for 8% of the time, Pallas kernels for 14%

profile of v2, /device:TPU:2, one launch (start us, length us, event | category | flops | bytes accessed | tf_op | source)
XLA Modules:
  0.0 65.1 jit_solution(11321936505975079370)
XLA Ops:
  0.6 7.6 %shard_map.76.merged_ref = bf16[32,32,896]{2,1,0:T(8,128)(2,1)} custom-call(s32[3,1,8,112]{3,2,1,0:T(8,128)} %bitcast.6, bf16[1,896,1024]{2,1,0:T(8,128)(2,1)} %base_hbm.1, bf16[3,1,896,1024]{3,2,1,0:T(8,128)(2,1)} %delta_ref.1), custom_call_target="tpu_custom_call" | custom-call | tf_op jit(solution)/shard_map/pallas_call | solution.py:114
  8.2 13.0 %all-to-all-start = ((bf16[32,32,896]{2,1,0:T(8,128)(2,1)}), bf16[32,32,896]{2,1,0:T(8,128)(2,1)S(1)}, u32[]{:S(2)}, u32[]{:S(2)}) async-start(bf16[32,32,896]{2,1,0:T(8,128)(2,1)} %shard_map.76.merged_ref), calls=%async_computation | async-start | bytes 3670016 | tf_op jit(solution)/shard_map/all_to_all | solution.py:206
  21.2 0.0 copy-start.2
  21.2 0.0 copy-start
  21.2 0.0 copy-start.1
  21.3 8.8 %shard_map.78 = (f32[8,128]{1,0:T(8,128)}, f32[8,128]{1,0:T(8,128)}) custom-call(s32[3,1,8,112]{3,2,1,0:T(8,128)} %bitcast.7, bf16[3,1,896,1024]{3,2,1,0:T(8,128)(2,1)} %delta_ref.1, bf16[32,32,896]{2,1,0:T(8,128)(2,1)} %shard_map.76.merged_ref), custom_call_target="tpu_custom_call" | custom-call | tf_op jit(solution)/shard_map/pallas_call | solution.py:162
  30.1 0.0 copy-done.2
  30.1 0.6 dynamic-slice
  31.3 1.3 %reduce_max.18 = f32[]{:T(128)} reduce(f32[8,128]{1,0:T(8,128)} %get-tuple-element.6, f32[]{:T(128)} %constant.8.clone.1), dimensions={0,1}, to_apply=%region_1.0 | reduce | flops 1023 | bytes 4104 | tf_op jit(solution)/shard_map/reduce_max | solution.py:210
  32.6 1.3 %reduce_sum.18 = f32[]{:T(128)} reduce(f32[8,128]{1,0:T(8,128)} %get-tuple-element.5, f32[]{:T(128)} %constant.3.clone.1), dimensions={0,1}, to_apply=%region_0.0 | reduce | flops 1023 | bytes 4104 | tf_op jit(solution)/shard_map/reduce_sum | solution.py:210
  33.9 1.4 %maximum_dynamic-update-slice_fusion = f32[16]{0:T(128)S(1)} fusion(f32[16]{0:T(128)S(1)} %broadcast, u32[]{:T(128)} %bitcast.3, f32[1]{0:T(128)} %bitcast.2, f32[1]{0:T(128)} %bitcast.1), kind=kLoop, calls=%fused_computation.2 | loop fusion | flops 2 | bytes 76
  35.3 14.9 %all-reduce = f32[16]{0:T(128)S(1)} all-reduce(f32[16]{0:T(128)S(1)} %maximum_dynamic-update-slice_fusion), channel_id=2, replica_groups=mesh['expert'=32,'mp'=8] {'mp'}, use_global_device_ids=true, to_apply=%add | all-reduce | flops 16 | bytes 128
  50.1 0.1 reshape.8
  50.2 0.7 %slice_reduce_fusion = (f32[]{:T(128)}, f32[]{:T(128)}) fusion(f32[8,2]{1,0:T(8,128)S(1)} %reshape.8), kind=kLoop, calls=%fused_computation | loop fusion | flops 14 | bytes 72 | tf_op jit(solution)/shard_map/reduce_max | solution.py:213
  51.6 10.4 %all-to-all-done.in_ref = bf16[32,32,896]{2,1,0:T(8,128)(2,1)S(1)} async-done(((bf16[32,32,896]{2,1,0:T(8,128)(2,1)}), bf16[32,32,896]{2,1,0:T(8,128)(2,1)S(1)}, u32[]{:S(2)}, u32[]{:S(2)}) %all-to-all-start) | async-done | bytes 1835040 | tf_op jit(solution)/shard_map/all_to_all | solution.py:206
  61.9 0.0 copy-done
  61.9 0.0 copy-done.1
  62.0 2.0 %shard_map.77 = bf16[32,32,896]{2,1,0:T(8,128)(2,1)} custom-call(s32[32]{0:T(128)S(1)} %copy-done, s32[32]{0:T(128)S(1)} %copy-done.1, bf16[32,32,896]{2,1,0:T(8,128)(2,1)S(1)} %all-to-all-done.in_ref), custom_call_target="tpu_custom_call" | custom-call | tf_op jit(solution)/shard_map/pallas_call | solution.py:189
  (1 shorter events, 0.0 us)
Async XLA Ops:
  8.2 53.7 %all-to-all-start = ((bf16[32,32,896]{2,1,0:T(8,128)(2,1)}), bf16[32,32,896]{2,1,0:T(8,128)(2,1)S(1)}, u32[]{:S(2)}, u32[]{:S(2)}) async-start(bf16[32,32,896]{2,1,0:T(8,128)(2,1)} %shard_map.76.merged_ref), calls=%async_computation | async-start | bytes 3670016 | tf_op jit(solution)/shard_map/all_to_all | solution.py:206
  21.2 8.9 %copy-start.2 = (u32[256]{0:T(256)S(1)}, u32[256]{0:T(256)}, u32[]{:S(2)}) copy-start(u32[256]{0:T(256)} %constant.16) | copy-start | bytes 3076
  21.2 40.7 %copy-start = (s32[32]{0:T(128)S(1)}, s32[32]{0:T(128)}, u32[]{:S(2)}) copy-start(s32[32]{0:T(128)} %order_ref.1) | copy-start | bytes 388
  21.2 40.7 %copy-start.1 = (s32[32]{0:T(128)S(1)}, s32[32]{0:T(128)}, u32[]{:S(2)}) copy-start(s32[32]{0:T(128)} %constant.10.clone.place_ref) | copy-start | bytes 388

commit v3 on v2

--- a/solution.py
+++ b/solution.py
@@ -80,16 +80,12 @@
     keep_copy.wait()
     for k in range(3):
         spread_ref[k] = spread_flags(k_buf[k, 0], columns)
-    fetch(1)
+    for i in range(1, n):
+        fetch(i)
 
     def chunk(i, carry):
         delta_copy(i).wait()
         base_copy(i).wait()
-
-        @pl.when(i + 2 < n)
-        def _():
-            fetch(i + 2)
-
         flag_rows = pl.ds(pl.multiple_of(i * blocks, blocks), blocks)
         for c in range(columns // LANES):
             cols = pl.ds(c * LANES, LANES)
@@ -174,6 +170,21 @@
     )(keep_turned, deltas, merged)
 
 
+def totals_kernel(both_ref, total_ref, largest_ref):
+    total_ref[0] = jnp.sum(both_ref[:, 0:1]) * (1.0 / math.sqrt(D * F))
+    largest_ref[0] = jnp.max(both_ref[:, 1:2])
+
+
+def totals(both):
+    one = jax.ShapeDtypeStruct((1,), jnp.float32)
+    return pl.pallas_call(
+        totals_kernel,
+        in_specs=[pl.BlockSpec(memory_space=pltpu.VMEM)],
+        out_specs=[pl.BlockSpec(memory_space=pltpu.SMEM)] * 2,
+        out_shape=[one, one],
+    )(both)
+
+
 def place_kernel(order_ref, place_ref, in_ref, out_ref, sems):
     def copy(s):
         return pltpu.make_async_copy(in_ref.at[place_ref[order_ref[s]]], out_ref.at[s], sems.at[s])
@@ -209,8 +220,9 @@
     sums, largest = figures(keep_turned, deltas, merged)
     here = jnp.stack([jnp.sum(sums), jnp.max(largest)])
     both = lax.all_gather(here, "mp")
+    total, largest = totals(both)
     serving = place(arranged, serve_order)
-    return (serving, both[:, 0].sum(0)[None] / math.sqrt(D * F), both[:, 1].max(0)[None])
+    return (serving, total, largest)
 
 
 def solution(mesh):

time: 66.1 us -> 64.9 us (0.982)
  between operations: 3.12 us -> 1.34 us
  Pallas kernels: 18.5 us -> 19.8 us
  other arithmetic: 4.61 us -> 3.93 us
    pallas_call x0 -> x1, Pallas kernels: none -> 1.32 us  [totals(): pl.pallas_call(totals_kernel, in_specs=[pl.BlockSpec(memory_space=pltpu.V...]
    reduce_max x1 -> x0, other arithmetic: 0.68 us -> none  [on_device(): both[:, 1].max(0)[None]]
  transfers between devices with their start and end apart: 1 -> 1, of which waited for: 1 -> 1; matrix products, arithmetic and copies ran while one was open for 8% -> 8% of each run, Pallas kernels for 14% -> 16%
where the time goes in v3:
time: 64.9 us; the launch traced here: 64 us
  Pallas kernels  19.8 us (31%)
  blocking collectives  14.9 us (23%)
  starting transfers between devices  13 us (20%)
  waiting for transfers between devices  9.79 us (15%)
  other arithmetic  3.93 us (6%)
  between operations  1.34 us (2%)
  local copies, waits for them, and re-layouts  1.28 us (2%)
    unnamed x1, blocking collectives  14.9 us
    all_to_all x1, starting transfers between devices, on_device(): lax.all_to_all(merged, 'expert', split_axis=0, concat_axis=0, tiled=True,...  13 us
    all_to_all x1, waiting for transfers between devices, on_device(): lax.all_to_all(merged, 'expert', split_axis=0, concat_axis=0, tiled=True,...  9.79 us
    pallas_call x1, Pallas kernels, figures(): pl.pallas_call(figures_kernel, grid=(rows // STEP,), in_specs=[pl.BlockSp...  8.84 us
    pallas_call x1, Pallas kernels, merge(): pl.pallas_call(merge_kernel, in_specs=[pl.BlockSpec(memory_space=pl.ANY)]...  7.6 us
    pallas_call x1, Pallas kernels, place(): pl.pallas_call(place_kernel, in_specs=[pl.BlockSpec(memory_space=pltpu.SM...  2.03 us
    unnamed x1, other arithmetic  1.37 us
    pallas_call x1, Pallas kernels, totals(): pl.pallas_call(totals_kernel, in_specs=[pl.BlockSpec(memory_space=pltpu.V...  1.32 us
  transfers between devices with their start and end apart: 1, of which 1 were waited for; matrix products, arithmetic and copies ran while one was open for 8% of the time, Pallas kernels for 16%

profile of v3, /device:TPU:2, one launch (start us, length us, event | category | flops | bytes accessed | tf_op | source)
XLA Modules:
  0.0 64.0 jit_solution(4086331039601250744)
XLA Ops:
  0.6 7.6 %shard_map.76.merged_ref = bf16[32,32,896]{2,1,0:T(8,128)(2,1)} custom-call(s32[3,1,8,112]{3,2,1,0:T(8,128)} %bitcast.4, bf16[1,896,1024]{2,1,0:T(8,128)(2,1)} %base_hbm.1, bf16[3,1,896,1024]{3,2,1,0:T(8,128)(2,1)} %delta_ref.1), custom_call_target="tpu_custom_call" | custom-call | tf_op jit(solution)/shard_map/pallas_call | solution.py:110
  8.2 13.0 %all-to-all-start = ((bf16[32,32,896]{2,1,0:T(8,128)(2,1)}), bf16[32,32,896]{2,1,0:T(8,128)(2,1)S(1)}, u32[]{:S(2)}, u32[]{:S(2)}) async-start(bf16[32,32,896]{2,1,0:T(8,128)(2,1)} %shard_map.76.merged_ref), calls=%async_computation | async-start | bytes 3670016 | tf_op jit(solution)/shard_map/all_to_all | solution.py:217
  21.2 0.0 copy-start.2
  21.2 0.0 copy-start
  21.2 0.0 copy-start.1
  21.2 8.8 %shard_map.78 = (f32[8,128]{1,0:T(8,128)}, f32[8,128]{1,0:T(8,128)}) custom-call(s32[3,1,8,112]{3,2,1,0:T(8,128)} %bitcast.5, bf16[3,1,896,1024]{3,2,1,0:T(8,128)(2,1)} %delta_ref.1, bf16[32,32,896]{2,1,0:T(8,128)(2,1)} %shard_map.76.merged_ref), custom_call_target="tpu_custom_call" | custom-call | tf_op jit(solution)/shard_map/pallas_call | solution.py:158
  30.1 0.0 copy-done.2
  30.1 0.6 dynamic-slice
  31.3 1.3 %reduce_max.9 = f32[]{:T(128)} reduce(f32[8,128]{1,0:T(8,128)} %get-tuple-element.8, f32[]{:T(128)} %constant.2.clone.1), dimensions={0,1}, to_apply=%region_1.0 | reduce | flops 1023 | bytes 4104 | tf_op jit(solution)/shard_map/reduce_max | solution.py:221
  32.6 1.3 %reduce_sum.9 = f32[]{:T(128)} reduce(f32[8,128]{1,0:T(8,128)} %get-tuple-element.7, f32[]{:T(128)} %constant.1.clone.1), dimensions={0,1}, to_apply=%region_0.0 | reduce | flops 1023 | bytes 4104 | tf_op jit(solution)/shard_map/reduce_sum | solution.py:221
  33.9 1.4 %maximum_dynamic-update-slice_fusion = f32[16]{0:T(128)S(1)} fusion(f32[16]{0:T(128)S(1)} %broadcast, u32[]{:T(128)} %bitcast.3, f32[1]{0:T(128)} %bitcast.2, f32[1]{0:T(128)} %bitcast.1), kind=kLoop, calls=%fused_computation | loop fusion | flops 2 | bytes 76
  35.3 14.9 %all-reduce = f32[16]{0:T(128)S(1)} all-reduce(f32[16]{0:T(128)S(1)} %maximum_dynamic-update-slice_fusion), channel_id=2, replica_groups=mesh['expert'=32,'mp'=8] {'mp'}, use_global_device_ids=true, to_apply=%add | all-reduce | flops 16 | bytes 128
  50.1 0.7 %reshape.6.both_ref = f32[8,2]{1,0:T(8,128)} reshape(f32[16]{0:T(128)S(1)} %all-reduce) | data formatting | bytes 128 | tf_op jit(solution)/shard_map/all_gather | solution.py:222
  50.8 1.3 %shard_map.79 = (f32[1]{0:T(128)}, f32[1]{0:T(128)}) custom-call(f32[8,2]{1,0:T(8,128)} %reshape.6.both_ref), custom_call_target="tpu_custom_call" | custom-call | tf_op jit(solution)/shard_map/pallas_call | solution.py:180
  52.1 9.8 %all-to-all-done.in_ref = bf16[32,32,896]{2,1,0:T(8,128)(2,1)S(1)} async-done(((bf16[32,32,896]{2,1,0:T(8,128)(2,1)}), bf16[32,32,896]{2,1,0:T(8,128)(2,1)S(1)}, u32[]{:S(2)}, u32[]{:S(2)}) %all-to-all-start) | async-done | bytes 1835040 | tf_op jit(solution)/shard_map/all_to_all | solution.py:217
  61.9 0.0 copy-done
  61.9 0.0 copy-done.1
  61.9 2.0 %shard_map.77 = bf16[32,32,896]{2,1,0:T(8,128)(2,1)} custom-call(s32[32]{0:T(128)S(1)} %copy-done, s32[32]{0:T(128)S(1)} %copy-done.1, bf16[32,32,896]{2,1,0:T(8,128)(2,1)S(1)} %all-to-all-done.in_ref), custom_call_target="tpu_custom_call" | custom-call | tf_op jit(solution)/shard_map/pallas_call | solution.py:200
  (1 shorter events, 0.0 us)
Async XLA Ops:
  8.2 53.7 %all-to-all-start = ((bf16[32,32,896]{2,1,0:T(8,128)(2,1)}), bf16[32,32,896]{2,1,0:T(8,128)(2,1)S(1)}, u32[]{:S(2)}, u32[]{:S(2)}) async-start(bf16[32,32,896]{2,1,0:T(8,128)(2,1)} %shard_map.76.merged_ref), calls=%async_computation | async-start | bytes 3670016 | tf_op jit(solution)/shard_map/all_to_all | solution.py:217
  21.2 8.9 %copy-start.2 = (u32[256]{0:T(256)S(1)}, u32[256]{0:T(256)}, u32[]{:S(2)}) copy-start(u32[256]{0:T(256)} %constant.12) | copy-start | bytes 3076
  21.2 40.7 %copy-start = (s32[32]{0:T(128)S(1)}, s32[32]{0:T(128)}, u32[]{:S(2)}) copy-start(s32[32]{0:T(128)} %order_ref.1) | copy-start | bytes 388
  21.2 40.7 %copy-start.1 = (s32[32]{0:T(128)S(1)}, s32[32]{0:T(128)}, u32[]{:S(2)}) copy-start(s32[32]{0:T(128)} %constant.6.clone.place_ref) | copy-start | bytes 388

commit v4 on v3

--- a/solution.py
+++ b/solution.py
@@ -12,14 +12,25 @@
 LANES = 128
 STEP = 128
 ORDER = [
-    19, 28, 1, 17, 12, 22, 16, 30, 15, 23, 11, 24, 6, 9, 31, 14,
-    25, 4, 26, 2, 27, 13, 0, 5, 18, 7, 3, 29, 20, 21, 8, 10,
+    19, 28, 1, 17, 12, 22, 16, 30, 15, 6, 9, 31, 14, 25, 4, 26,
+    2, 27, 13, 0, 5, 23, 11, 24, 18, 7, 3, 29, 20, 21, 8, 10,
 ]
 PLACE_OF = [ORDER.index(e) for e in range(32)]
 VMEM_BYTES = 60 * 2**20
 
 
-def spread_flags(flags, columns):
+def spread_flags(flags_ref, spread_ref, columns):
+    for k in range(3):
+        spread = spread_over_lanes(flags_ref[k, 0], columns)
+        for c in range(columns // LANES):
+            spread_ref[k, c, pl.ds(0, spread.shape[0])] = spread[:, c * LANES : (c + 1) * LANES]
+
+
+def spread_scratch(rows, columns):
+    return pltpu.VMEM((3, columns // LANES, rows // 8 + 8, LANES), jnp.float32)
+
+
+def spread_over_lanes(flags, columns):
     lane_block = lax.broadcasted_iota(jnp.int32, (flags.shape[0], columns), 1) // LANES
     own_block = lax.broadcasted_iota(jnp.int32, (flags.shape[0], columns), 0)
     expand = (lane_block == own_block).astype(jnp.float32)
@@ -42,12 +53,14 @@
     return jnp.where(least > 0, s * (1.0 / 3.0), few)
 
 
-def trimmed_tile(delta_at, flags_at):
+def trimmed_tile(delta_at, spread_ref, column_block, first_block):
     out = []
     for k in range(3):
         d = delta_at(k).astype(jnp.float32)
-        rows = d.shape[0]
-        out.append(d.reshape(rows // 8, 8, LANES) * flags_at(k)[:, None, :])
+        blocks = d.shape[0] // 8
+        d = d.reshape(blocks, 8, LANES)
+        kept = [spread_ref[k, column_block, pl.ds(first_block + r, 8, stride=0)] for r in range(blocks)]
+        out.append(jnp.stack([d[r] * kept[r] for r in range(blocks)]))
     return out
 
 
@@ -78,18 +91,16 @@
     keep_copy.start()
     fetch(0)
     keep_copy.wait()
-    for k in range(3):
-        spread_ref[k] = spread_flags(k_buf[k, 0], columns)
+    spread_flags(k_buf, spread_ref, columns)
     for i in range(1, n):
         fetch(i)
 
     def chunk(i, carry):
         delta_copy(i).wait()
         base_copy(i).wait()
-        flag_rows = pl.ds(pl.multiple_of(i * blocks, blocks), blocks)
         for c in range(columns // LANES):
             cols = pl.ds(c * LANES, LANES)
-            t = trimmed_tile(lambda k: d_buf[k, rows_of(i), cols], lambda k: spread_ref[k, flag_rows, cols])
+            t = trimmed_tile(lambda k: d_buf[k, rows_of(i), cols], spread_ref, c, i * blocks)
             base = b_buf[rows_of(i), cols].astype(jnp.float32).reshape(blocks, 8, LANES)
             merged = (base + voted_update(t)).reshape(STEP, LANES).astype(jnp.bfloat16)
             turned = merged.T.reshape(4, LANES // 4, STEP)
@@ -117,7 +128,7 @@
             pltpu.VMEM((rows, columns), jnp.bfloat16),
             pltpu.VMEM((n, slots, columns // slots, STEP), jnp.bfloat16),
             pltpu.VMEM(keep_turned.shape, jnp.int32),
-            pltpu.VMEM((3, rows // 8, columns), jnp.float32),
+            spread_scratch(rows, columns),
             pltpu.SemaphoreType.DMA((n, 2)),
             pltpu.SemaphoreType.DMA((n,)),
             pltpu.SemaphoreType.DMA,
@@ -135,14 +146,12 @@
     def _():
         sums_ref[...] = jnp.zeros_like(sums_ref)
         largest_ref[...] = jnp.zeros_like(largest_ref)
-        for k in range(3):
-            spread_ref[k] = spread_flags(keep_ref[k, 0], columns)
-
-    flag_rows = pl.ds(pl.multiple_of(step * blocks, blocks), blocks)
+        spread_flags(keep_ref, spread_ref, columns)
+
     largest = largest_ref[...]
     for c in range(columns // LANES):
         cols = pl.ds(c * LANES, LANES)
-        t = trimmed_tile(lambda k: delta_ref[k, 0, :, cols], lambda k: spread_ref[k, flag_rows, cols])
+        t = trimmed_tile(lambda k: delta_ref[k, 0, :, cols], spread_ref, c, step * blocks)
         largest = jnp.maximum(largest, jnp.abs(voted_update(t)).max(axis=0))
     largest_ref[...] = largest
     total = sums_ref[...]
@@ -165,7 +174,7 @@
         ],
         out_specs=[pl.BlockSpec((8, LANES), lambda i: (0, 0))] * 2,
         out_shape=[jax.ShapeDtypeStruct((8, LANES), jnp.float32)] * 2,
-        scratch_shapes=[pltpu.VMEM((3, rows // 8, columns), jnp.float32)],
+        scratch_shapes=[spread_scratch(rows, columns)],
         compiler_params=pltpu.CompilerParams(vmem_limit_bytes=VMEM_BYTES),
     )(keep_turned, deltas, merged)
 

time: 64.9 us -> 63.4 us (0.977)
  Pallas kernels: 19.8 us -> 18.9 us
    pallas_call x1, Pallas kernels: 7.6 us -> 6.83 us  [merge(): pl.pallas_call(merge_kernel, in_specs=[pl.BlockSpec(memory_space=pl.ANY)]...]
where the time goes in v4:
time: 63.4 us; the launch traced here: 62.6 us
  Pallas kernels  18.9 us (30%)
  blocking collectives  14.6 us (23%)
  starting transfers between devices  13 us (21%)
  waiting for transfers between devices  9.63 us (15%)
  other arithmetic  3.93 us (6%)
  between operations  1.34 us (2%)
  local copies, waits for them, and re-layouts  1.28 us (2%)
    unnamed x1, blocking collectives  14.6 us
    all_to_all x1, starting transfers between devices, on_device(): lax.all_to_all(merged, 'expert', split_axis=0, concat_axis=0, tiled=True,...  13 us
    all_to_all x1, waiting for transfers between devices, on_device(): lax.all_to_all(merged, 'expert', split_axis=0, concat_axis=0, tiled=True,...  9.63 us
    pallas_call x1, Pallas kernels, figures(): pl.pallas_call(figures_kernel, grid=(rows // STEP,), in_specs=[pl.BlockSp...  8.68 us
    pallas_call x1, Pallas kernels, merge(): pl.pallas_call(merge_kernel, in_specs=[pl.BlockSpec(memory_space=pl.ANY)]...  6.83 us
    pallas_call x1, Pallas kernels, place(): pl.pallas_call(place_kernel, in_specs=[pl.BlockSpec(memory_space=pltpu.SM...  2.03 us
    unnamed x1, other arithmetic  1.37 us
    pallas_call x1, Pallas kernels, totals(): pl.pallas_call(totals_kernel, in_specs=[pl.BlockSpec(memory_space=pltpu.V...  1.32 us
  transfers between devices with their start and end apart: 1, of which 1 were waited for; matrix products, arithmetic and copies ran while one was open for 8% of the time, Pallas kernels for 16%

profile of v4, /device:TPU:2, one launch (start us, length us, event | category | flops | bytes accessed | tf_op | source)
XLA Modules:
  0.0 62.6 jit_solution(4628655562481081226)
XLA Ops:
  0.6 6.8 %shard_map.76.merged_ref = bf16[32,32,896]{2,1,0:T(8,128)(2,1)} custom-call(s32[3,1,8,112]{3,2,1,0:T(8,128)} %bitcast.4, bf16[1,896,1024]{2,1,0:T(8,128)(2,1)} %base_hbm.1, bf16[3,1,896,1024]{3,2,1,0:T(8,128)(2,1)} %delta_ref.1), custom_call_target="tpu_custom_call" | custom-call | tf_op jit(solution)/shard_map/pallas_call | solution.py:121
  7.5 13.0 %all-to-all-start = ((bf16[32,32,896]{2,1,0:T(8,128)(2,1)}), bf16[32,32,896]{2,1,0:T(8,128)(2,1)S(1)}, u32[]{:S(2)}, u32[]{:S(2)}) async-start(bf16[32,32,896]{2,1,0:T(8,128)(2,1)} %shard_map.76.merged_ref), calls=%async_computation | async-start | bytes 3670016 | tf_op jit(solution)/shard_map/all_to_all | solution.py:226
  20.4 0.0 copy-start.2
  20.5 0.0 copy-start
  20.5 0.0 copy-start.1
  20.5 8.7 %shard_map.78 = (f32[8,128]{1,0:T(8,128)}, f32[8,128]{1,0:T(8,128)}) custom-call(s32[3,1,8,112]{3,2,1,0:T(8,128)} %bitcast.5, bf16[3,1,896,1024]{3,2,1,0:T(8,128)(2,1)} %delta_ref.1, bf16[32,32,896]{2,1,0:T(8,128)(2,1)} %shard_map.76.merged_ref), custom_call_target="tpu_custom_call" | custom-call | tf_op jit(solution)/shard_map/pallas_call | solution.py:167
  29.2 0.0 copy-done.2
  29.2 0.6 dynamic-slice
  30.4 1.3 %reduce_max.9 = f32[]{:T(128)} reduce(f32[8,128]{1,0:T(8,128)} %get-tuple-element.8, f32[]{:T(128)} %constant.2.clone.1), dimensions={0,1}, to_apply=%region_1.0 | reduce | flops 1023 | bytes 4104 | tf_op jit(solution)/shard_map/reduce_max | solution.py:230
  31.7 1.3 %reduce_sum.9 = f32[]{:T(128)} reduce(f32[8,128]{1,0:T(8,128)} %get-tuple-element.7, f32[]{:T(128)} %constant.1.clone.1), dimensions={0,1}, to_apply=%region_0.0 | reduce | flops 1023 | bytes 4104 | tf_op jit(solution)/shard_map/reduce_sum | solution.py:230
  33.0 1.4 %maximum_dynamic-update-slice_fusion = f32[16]{0:T(128)S(1)} fusion(f32[16]{0:T(128)S(1)} %broadcast, u32[]{:T(128)} %bitcast.3, f32[1]{0:T(128)} %bitcast.2, f32[1]{0:T(128)} %bitcast.1), kind=kLoop, calls=%fused_computation | loop fusion | flops 2 | bytes 76
  34.3 14.6 %all-reduce = f32[16]{0:T(128)S(1)} all-reduce(f32[16]{0:T(128)S(1)} %maximum_dynamic-update-slice_fusion), channel_id=2, replica_groups=mesh['expert'=32,'mp'=8] {'mp'}, use_global_device_ids=true, to_apply=%add | all-reduce | flops 16 | bytes 128
  48.9 0.7 %reshape.6.both_ref = f32[8,2]{1,0:T(8,128)} reshape(f32[16]{0:T(128)S(1)} %all-reduce) | data formatting | bytes 128 | tf_op jit(solution)/shard_map/all_gather | solution.py:231
  49.6 1.3 %shard_map.79 = (f32[1]{0:T(128)}, f32[1]{0:T(128)}) custom-call(f32[8,2]{1,0:T(8,128)} %reshape.6.both_ref), custom_call_target="tpu_custom_call" | custom-call | tf_op jit(solution)/shard_map/pallas_call | solution.py:189
  50.9 9.6 %all-to-all-done.in_ref = bf16[32,32,896]{2,1,0:T(8,128)(2,1)S(1)} async-done(((bf16[32,32,896]{2,1,0:T(8,128)(2,1)}), bf16[32,32,896]{2,1,0:T(8,128)(2,1)S(1)}, u32[]{:S(2)}, u32[]{:S(2)}) %all-to-all-start) | async-done | bytes 1835040 | tf_op jit(solution)/shard_map/all_to_all | solution.py:226
  60.5 0.0 copy-done
  60.5 0.0 copy-done.1
  60.5 2.0 %shard_map.77 = bf16[32,32,896]{2,1,0:T(8,128)(2,1)} custom-call(s32[32]{0:T(128)S(1)} %copy-done, s32[32]{0:T(128)S(1)} %copy-done.1, bf16[32,32,896]{2,1,0:T(8,128)(2,1)S(1)} %all-to-all-done.in_ref), custom_call_target="tpu_custom_call" | custom-call | tf_op jit(solution)/shard_map/pallas_call | solution.py:209
  (1 shorter events, 0.0 us)
Async XLA Ops:
  7.5 53.1 %all-to-all-start = ((bf16[32,32,896]{2,1,0:T(8,128)(2,1)}), bf16[32,32,896]{2,1,0:T(8,128)(2,1)S(1)}, u32[]{:S(2)}, u32[]{:S(2)}) async-start(bf16[32,32,896]{2,1,0:T(8,128)(2,1)} %shard_map.76.merged_ref), calls=%async_computation | async-start | bytes 3670016 | tf_op jit(solution)/shard_map/all_to_all | solution.py:226
  20.4 8.7 %copy-start.2 = (u32[256]{0:T(256)S(1)}, u32[256]{0:T(256)}, u32[]{:S(2)}) copy-start(u32[256]{0:T(256)} %constant.12) | copy-start | bytes 3076
  20.5 40.1 %copy-start = (s32[32]{0:T(128)S(1)}, s32[32]{0:T(128)}, u32[]{:S(2)}) copy-start(s32[32]{0:T(128)} %order_ref.1) | copy-start | bytes 388
  20.5 40.1 %copy-start.1 = (s32[32]{0:T(128)S(1)}, s32[32]{0:T(128)}, u32[]{:S(2)}) copy-start(s32[32]{0:T(128)} %constant.6.clone.place_ref) | copy-start | bytes 388

commit v5 on v4

--- a/solution.py
+++ b/solution.py
@@ -179,24 +179,30 @@
     )(keep_turned, deltas, merged)
 
 
-def totals_kernel(both_ref, total_ref, largest_ref):
+def totals_kernel(both_ref, order_ref, place_ref, total_ref, largest_ref, source_ref):
+    for s in range(source_ref.shape[0]):
+        source_ref[s] = place_ref[order_ref[s]]
     total_ref[0] = jnp.sum(both_ref[:, 0:1]) * (1.0 / math.sqrt(D * F))
     largest_ref[0] = jnp.max(both_ref[:, 1:2])
 
 
-def totals(both):
+def totals(both, serve_order):
     one = jax.ShapeDtypeStruct((1,), jnp.float32)
     return pl.pallas_call(
         totals_kernel,
-        in_specs=[pl.BlockSpec(memory_space=pltpu.VMEM)],
-        out_specs=[pl.BlockSpec(memory_space=pltpu.SMEM)] * 2,
-        out_shape=[one, one],
-    )(both)
-
-
-def place_kernel(order_ref, place_ref, in_ref, out_ref, sems):
+        in_specs=[
+            pl.BlockSpec(memory_space=pltpu.VMEM),
+            pl.BlockSpec(memory_space=pltpu.SMEM),
+            pl.BlockSpec(memory_space=pltpu.SMEM),
+        ],
+        out_specs=[pl.BlockSpec(memory_space=pltpu.SMEM)] * 3,
+        out_shape=[one, one, pltpu.SMEM(serve_order.shape, jnp.int32)],
+    )(both, serve_order, jnp.array(PLACE_OF, jnp.int32))
+
+
+def place_kernel(source_ref, in_ref, out_ref, sems):
     def copy(s):
-        return pltpu.make_async_copy(in_ref.at[place_ref[order_ref[s]]], out_ref.at[s], sems.at[s])
+        return pltpu.make_async_copy(in_ref.at[source_ref[s]], out_ref.at[s], sems.at[s])
 
     for s in range(out_ref.shape[0]):
         copy(s).start()
@@ -204,12 +210,11 @@
         copy(s).wait()
 
 
-def place(arranged, serve_order):
+def place(arranged, source):
     n = arranged.shape[0]
     return pl.pallas_call(
         place_kernel,
         in_specs=[
-            pl.BlockSpec(memory_space=pltpu.SMEM),
             pl.BlockSpec(memory_space=pltpu.SMEM),
             pl.BlockSpec(memory_space=pl.ANY),
         ],
@@ -217,7 +222,7 @@
         out_shape=jax.ShapeDtypeStruct(arranged.shape, arranged.dtype),
         scratch_shapes=[pltpu.SemaphoreType.DMA((n,))],
         compiler_params=pltpu.CompilerParams(vmem_limit_bytes=4 * 2**20),
-    )(serve_order, jnp.array(PLACE_OF, jnp.int32), arranged)
+    )(source, arranged)
 
 
 def on_device(base_weights, deltas, keep_flags, serve_order):
@@ -229,8 +234,8 @@
     sums, largest = figures(keep_turned, deltas, merged)
     here = jnp.stack([jnp.sum(sums), jnp.max(largest)])
     both = lax.all_gather(here, "mp")
-    total, largest = totals(both)
-    serving = place(arranged, serve_order)
+    total, largest, source = totals(both, serve_order)
+    serving = place(arranged, source)
     return (serving, total, largest)
 
 

time: 63.4 us -> 62.8 us (level)
  no operation moved by 1% of the time
where the time goes in v5:
time: 62.8 us; the launch traced here: 62 us
  Pallas kernels  18.4 us (29%)
  blocking collectives  14.6 us (23%)
  starting transfers between devices  13 us (21%)
  waiting for transfers between devices  9.58 us (15%)
  other arithmetic  3.93 us (6%)
  between operations  1.33 us (2%)
  local copies, waits for them, and re-layouts  1.27 us (2%)
    unnamed x1, blocking collectives  14.6 us
    all_to_all x1, starting transfers between devices, on_device(): lax.all_to_all(merged, 'expert', split_axis=0, concat_axis=0, tiled=True,...  13 us
    all_to_all x1, waiting for transfers between devices, on_device(): lax.all_to_all(merged, 'expert', split_axis=0, concat_axis=0, tiled=True,...  9.58 us
    pallas_call x1, Pallas kernels, figures(): pl.pallas_call(figures_kernel, grid=(rows // STEP,), in_specs=[pl.BlockSp...  8.63 us
    pallas_call x1, Pallas kernels, merge(): pl.pallas_call(merge_kernel, in_specs=[pl.BlockSpec(memory_space=pl.ANY)]...  6.83 us
    pallas_call x1, Pallas kernels, place(): pl.pallas_call(place_kernel, in_specs=[pl.BlockSpec(memory_space=pltpu.SM...  1.48 us
    pallas_call x1, Pallas kernels, totals(): pl.pallas_call(totals_kernel, in_specs=[pl.BlockSpec(memory_space=pltpu.V...  1.45 us
    unnamed x1, other arithmetic  1.37 us
  transfers between devices with their start and end apart: 1, of which 1 were waited for; matrix products, arithmetic and copies ran while one was open for 8% of the time, Pallas kernels for 16%

profile of v5, /device:TPU:2, one launch (start us, length us, event | category | flops | bytes accessed | tf_op | source)
XLA Modules:
  0.0 62.0 jit_solution(13578356089937882131)
XLA Ops:
  0.6 6.8 %shard_map.76.merged_ref = bf16[32,32,896]{2,1,0:T(8,128)(2,1)} custom-call(s32[3,1,8,112]{3,2,1,0:T(8,128)} %bitcast.4, bf16[1,896,1024]{2,1,0:T(8,128)(2,1)} %base_hbm.1, bf16[3,1,896,1024]{3,2,1,0:T(8,128)(2,1)} %delta_ref.1), custom_call_target="tpu_custom_call" | custom-call | tf_op jit(solution)/shard_map/pallas_call | solution.py:121
  7.5 13.0 %all-to-all-start = ((bf16[32,32,896]{2,1,0:T(8,128)(2,1)}), bf16[32,32,896]{2,1,0:T(8,128)(2,1)S(1)}, u32[]{:S(2)}, u32[]{:S(2)}) async-start(bf16[32,32,896]{2,1,0:T(8,128)(2,1)} %shard_map.76.merged_ref), calls=%async_computation | async-start | bytes 3670016 | tf_op jit(solution)/shard_map/all_to_all | solution.py:231
  20.4 0.0 copy-start
  20.5 8.6 %shard_map.77 = (f32[8,128]{1,0:T(8,128)}, f32[8,128]{1,0:T(8,128)}) custom-call(s32[3,1,8,112]{3,2,1,0:T(8,128)} %bitcast.5, bf16[3,1,896,1024]{3,2,1,0:T(8,128)(2,1)} %delta_ref.1, bf16[32,32,896]{2,1,0:T(8,128)(2,1)} %shard_map.76.merged_ref), custom_call_target="tpu_custom_call" | custom-call | tf_op jit(solution)/shard_map/pallas_call | solution.py:167
  29.1 0.0 copy-done
  29.1 0.6 dynamic-slice
  30.3 1.3 %reduce_max.9 = f32[]{:T(128)} reduce(f32[8,128]{1,0:T(8,128)} %get-tuple-element.9, f32[]{:T(128)} %constant.2.clone.1), dimensions={0,1}, to_apply=%region_1.0 | reduce | flops 1023 | bytes 4104 | tf_op jit(solution)/shard_map/reduce_max | solution.py:235
  31.6 1.3 %reduce_sum.9 = f32[]{:T(128)} reduce(f32[8,128]{1,0:T(8,128)} %get-tuple-element.8, f32[]{:T(128)} %constant.1.clone.1), dimensions={0,1}, to_apply=%region_0.0 | reduce | flops 1023 | bytes 4104 | tf_op jit(solution)/shard_map/reduce_sum | solution.py:235
  32.9 1.4 %maximum_dynamic-update-slice_fusion = f32[16]{0:T(128)S(1)} fusion(f32[16]{0:T(128)S(1)} %broadcast, u32[]{:T(128)} %bitcast.3, f32[1]{0:T(128)} %bitcast.2, f32[1]{0:T(128)} %bitcast.1), kind=kLoop, calls=%fused_computation | loop fusion | flops 2 | bytes 76
  34.2 14.6 %all-reduce = f32[16]{0:T(128)S(1)} all-reduce(f32[16]{0:T(128)S(1)} %maximum_dynamic-update-slice_fusion), channel_id=2, replica_groups=mesh['expert'=32,'mp'=8] {'mp'}, use_global_device_ids=true, to_apply=%add | all-reduce | flops 16 | bytes 128
  48.8 0.7 %reshape.6.both_ref = f32[8,2]{1,0:T(8,128)} reshape(f32[16]{0:T(128)S(1)} %all-reduce) | data formatting | bytes 128 | tf_op jit(solution)/shard_map/all_gather | solution.py:236
  49.5 1.4 %shard_map.78 = (f32[1]{0:T(128)}, f32[1]{0:T(128)}, s32[32]{0:T(128)S(4)}) custom-call(f32[8,2]{1,0:T(8,128)} %reshape.6.both_ref, s32[32]{0:T(128)} %order_ref.1, s32[32]{0:T(128)} %constant.6.clone.place_ref), custom_call_target="tpu_custom_call" | custom-call | tf_op jit(solution)/shard_map/pallas_call | solution.py:191
  51.0 9.6 %all-to-all-done.in_ref = bf16[32,32,896]{2,1,0:T(8,128)(2,1)S(1)} async-done(((bf16[32,32,896]{2,1,0:T(8,128)(2,1)}), bf16[32,32,896]{2,1,0:T(8,128)(2,1)S(1)}, u32[]{:S(2)}, u32[]{:S(2)}) %all-to-all-start) | async-done | bytes 1835040 | tf_op jit(solution)/shard_map/all_to_all | solution.py:231
  60.5 1.5 %shard_map.79 = bf16[32,32,896]{2,1,0:T(8,128)(2,1)} custom-call(s32[32]{0:T(128)S(4)} %get-tuple-element.10.source_ref, bf16[32,32,896]{2,1,0:T(8,128)(2,1)S(1)} %all-to-all-done.in_ref), custom_call_target="tpu_custom_call" | custom-call | tf_op jit(solution)/shard_map/pallas_call | solution.py:215
  (1 shorter events, 0.0 us)
Async XLA Ops:
  7.5 53.1 %all-to-all-start = ((bf16[32,32,896]{2,1,0:T(8,128)(2,1)}), bf16[32,32,896]{2,1,0:T(8,128)(2,1)S(1)}, u32[]{:S(2)}, u32[]{:S(2)}) async-start(bf16[32,32,896]{2,1,0:T(8,128)(2,1)} %shard_map.76.merged_ref), calls=%async_computation | async-start | bytes 3670016 | tf_op jit(solution)/shard_map/all_to_all | solution.py:231
  20.4 8.6 %copy-start = (u32[256]{0:T(256)S(1)}, u32[256]{0:T(256)}, u32[]{:S(2)}) copy-start(u32[256]{0:T(256)} %constant.12) | copy-start | bytes 3076

commit v6 on v5

--- a/solution.py
+++ b/solution.py
@@ -12,7 +12,7 @@
 LANES = 128
 STEP = 128
 ORDER = [
-    19, 28, 1, 17, 12, 22, 16, 30, 15, 6, 9, 31, 14, 25, 4, 26,
+    19, 28, 1, 17, 12, 22, 16, 31, 9, 6, 15, 30, 14, 25, 4, 26,
     2, 27, 13, 0, 5, 23, 11, 24, 18, 7, 3, 29, 20, 21, 8, 10,
 ]
 PLACE_OF = [ORDER.index(e) for e in range(32)]

time: 62.8 us -> 62.5 us (level)
  no operation moved by 1% of the time
where the time goes in v6:
time: 62.5 us; the launch traced here: 62 us
  Pallas kernels  18.4 us (29%)
  blocking collectives  14.6 us (23%)
  starting transfers between devices  13 us (21%)
  waiting for transfers between devices  9.59 us (15%)
  other arithmetic  3.93 us (6%)
  between operations  1.33 us (2%)
  local copies, waits for them, and re-layouts  1.27 us (2%)
    unnamed x1, blocking collectives  14.6 us
    all_to_all x1, starting transfers between devices, on_device(): lax.all_to_all(merged, 'expert', split_axis=0, concat_axis=0, tiled=True,...  13 us
    all_to_all x1, waiting for transfers between devices, on_device(): lax.all_to_all(merged, 'expert', split_axis=0, concat_axis=0, tiled=True,...  9.59 us
    pallas_call x1, Pallas kernels, figures(): pl.pallas_call(figures_kernel, grid=(rows // STEP,), in_specs=[pl.BlockSp...  8.63 us
    pallas_call x1, Pallas kernels, merge(): pl.pallas_call(merge_kernel, in_specs=[pl.BlockSpec(memory_space=pl.ANY)]...  6.83 us
    pallas_call x1, Pallas kernels, place(): pl.pallas_call(place_kernel, in_specs=[pl.BlockSpec(memory_space=pltpu.SM...  1.48 us
    pallas_call x1, Pallas kernels, totals(): pl.pallas_call(totals_kernel, in_specs=[pl.BlockSpec(memory_space=pltpu.V...  1.45 us
    unnamed x1, other arithmetic  1.37 us
  transfers between devices with their start and end apart: 1, of which 1 were waited for; matrix products, arithmetic and copies ran while one was open for 8% of the time, Pallas kernels for 16%

profile of v6, /device:TPU:2, one launch (start us, length us, event | category | flops | bytes accessed | tf_op | source)
XLA Modules:
  0.0 62.0 jit_solution(12151288910097115563)
XLA Ops:
  0.6 6.8 %shard_map.76.merged_ref = bf16[32,32,896]{2,1,0:T(8,128)(2,1)} custom-call(s32[3,1,8,112]{3,2,1,0:T(8,128)} %bitcast.4, bf16[1,896,1024]{2,1,0:T(8,128)(2,1)} %base_hbm.1, bf16[3,1,896,1024]{3,2,1,0:T(8,128)(2,1)} %delta_ref.1), custom_call_target="tpu_custom_call" | custom-call | tf_op jit(solution)/shard_map/pallas_call | solution.py:121
  7.5 13.0 %all-to-all-start = ((bf16[32,32,896]{2,1,0:T(8,128)(2,1)}), bf16[32,32,896]{2,1,0:T(8,128)(2,1)S(1)}, u32[]{:S(2)}, u32[]{:S(2)}) async-start(bf16[32,32,896]{2,1,0:T(8,128)(2,1)} %shard_map.76.merged_ref), calls=%async_computation | async-start | bytes 3670016 | tf_op jit(solution)/shard_map/all_to_all | solution.py:231
  20.4 0.0 copy-start
  20.5 8.6 %shard_map.77 = (f32[8,128]{1,0:T(8,128)}, f32[8,128]{1,0:T(8,128)}) custom-call(s32[3,1,8,112]{3,2,1,0:T(8,128)} %bitcast.5, bf16[3,1,896,1024]{3,2,1,0:T(8,128)(2,1)} %delta_ref.1, bf16[32,32,896]{2,1,0:T(8,128)(2,1)} %shard_map.76.merged_ref), custom_call_target="tpu_custom_call" | custom-call | tf_op jit(solution)/shard_map/pallas_call | solution.py:167
  29.1 0.0 copy-done
  29.1 0.6 dynamic-slice
  30.3 1.3 %reduce_max.9 = f32[]{:T(128)} reduce(f32[8,128]{1,0:T(8,128)} %get-tuple-element.9, f32[]{:T(128)} %constant.2.clone.1), dimensions={0,1}, to_apply=%region_1.0 | reduce | flops 1023 | bytes 4104 | tf_op jit(solution)/shard_map/reduce_max | solution.py:235
  31.6 1.3 %reduce_sum.9 = f32[]{:T(128)} reduce(f32[8,128]{1,0:T(8,128)} %get-tuple-element.8, f32[]{:T(128)} %constant.1.clone.1), dimensions={0,1}, to_apply=%region_0.0 | reduce | flops 1023 | bytes 4104 | tf_op jit(solution)/shard_map/reduce_sum | solution.py:235
  32.9 1.4 %maximum_dynamic-update-slice_fusion = f32[16]{0:T(128)S(1)} fusion(f32[16]{0:T(128)S(1)} %broadcast, u32[]{:T(128)} %bitcast.3, f32[1]{0:T(128)} %bitcast.2, f32[1]{0:T(128)} %bitcast.1), kind=kLoop, calls=%fused_computation | loop fusion | flops 2 | bytes 76
  34.2 14.6 %all-reduce = f32[16]{0:T(128)S(1)} all-reduce(f32[16]{0:T(128)S(1)} %maximum_dynamic-update-slice_fusion), channel_id=2, replica_groups=mesh['expert'=32,'mp'=8] {'mp'}, use_global_device_ids=true, to_apply=%add | all-reduce | flops 16 | bytes 128
  48.8 0.7 %reshape.6.both_ref = f32[8,2]{1,0:T(8,128)} reshape(f32[16]{0:T(128)S(1)} %all-reduce) | data formatting | bytes 128 | tf_op jit(solution)/shard_map/all_gather | solution.py:236
  49.5 1.4 %shard_map.78 = (f32[1]{0:T(128)}, f32[1]{0:T(128)}, s32[32]{0:T(128)S(4)}) custom-call(f32[8,2]{1,0:T(8,128)} %reshape.6.both_ref, s32[32]{0:T(128)} %order_ref.1, s32[32]{0:T(128)} %constant.6.clone.place_ref), custom_call_target="tpu_custom_call" | custom-call | tf_op jit(solution)/shard_map/pallas_call | solution.py:191
  51.0 9.6 %all-to-all-done.in_ref = bf16[32,32,896]{2,1,0:T(8,128)(2,1)S(1)} async-done(((bf16[32,32,896]{2,1,0:T(8,128)(2,1)}), bf16[32,32,896]{2,1,0:T(8,128)(2,1)S(1)}, u32[]{:S(2)}, u32[]{:S(2)}) %all-to-all-start) | async-done | bytes 1835040 | tf_op jit(solution)/shard_map/all_to_all | solution.py:231
  60.6 1.5 %shard_map.79 = bf16[32,32,896]{2,1,0:T(8,128)(2,1)} custom-call(s32[32]{0:T(128)S(4)} %get-tuple-element.10.source_ref, bf16[32,32,896]{2,1,0:T(8,128)(2,1)S(1)} %all-to-all-done.in_ref), custom_call_target="tpu_custom_call" | custom-call | tf_op jit(solution)/shard_map/pallas_call | solution.py:215
  (1 shorter events, 0.0 us)
Async XLA Ops:
  7.5 53.1 %all-to-all-start = ((bf16[32,32,896]{2,1,0:T(8,128)(2,1)}), bf16[32,32,896]{2,1,0:T(8,128)(2,1)S(1)}, u32[]{:S(2)}, u32[]{:S(2)}) async-start(bf16[32,32,896]{2,1,0:T(8,128)(2,1)} %shard_map.76.merged_ref), calls=%async_computation | async-start | bytes 3670016 | tf_op jit(solution)/shard_map/all_to_all | solution.py:231
  20.4 8.6 %copy-start = (u32[256]{0:T(256)S(1)}, u32[256]{0:T(256)}, u32[]{:S(2)}) copy-start(u32[256]{0:T(256)} %constant.12) | copy-start | bytes 3076

commit v7 on v6

--- a/solution.py
+++ b/solution.py
@@ -43,14 +43,19 @@
 
 
 def voted_update(t):
+    t = [x.reshape(x.shape[0] * 8, LANES) for x in t]
     s = t[0] + t[1] + t[2]
-    sign = jnp.where(s > 0, 1.0, jnp.where(s < 0, -1.0, 0.0))
-    a, b, c = (x * sign for x in t)
+    direction = s.astype(jnp.bfloat16)
+    zero, one = jnp.bfloat16(0), jnp.bfloat16(1)
+    sign = jnp.where(direction > zero, one, jnp.where(direction < zero, -one, zero))
+    a, b, c = (x.astype(jnp.bfloat16) * sign for x in t)
     low, high = jnp.minimum(a, b), jnp.maximum(a, b)
     most, least = jnp.maximum(high, c), jnp.minimum(low, c)
     middle = jnp.maximum(low, jnp.minimum(high, c))
-    few = jnp.where(middle > 0, (most + middle) * 0.5, most) * sign
-    return jnp.where(least > 0, s * (1.0 / 3.0), few)
+    second = jnp.where(middle > zero, middle, most)
+    few = ((most * sign).astype(jnp.float32) + (second * sign).astype(jnp.float32)) * 0.5
+    update = jnp.where(least.astype(jnp.float32) > 0, s * (1.0 / 3.0), few)
+    return update.reshape(update.shape[0] // 8, 8, LANES)
 
 
 def trimmed_tile(delta_at, spread_ref, column_block, first_block):

time: 62.5 us -> 62.3 us (level)
  Pallas kernels: 18.4 us -> 17.7 us
where the time goes in v7:
time: 62.3 us; the launch traced here: 61.8 us
  Pallas kernels  17.7 us (28%)
  blocking collectives  14.6 us (23%)
  starting transfers between devices  13 us (21%)
  waiting for transfers between devices  10.1 us (16%)
  other arithmetic  3.93 us (6%)
  between operations  1.33 us (2%)
  local copies, waits for them, and re-layouts  1.27 us (2%)
    unnamed x1, blocking collectives  14.6 us
    all_to_all x1, starting transfers between devices, on_device(): lax.all_to_all(merged, 'expert', split_axis=0, concat_axis=0, tiled=True,...  13 us
    all_to_all x1, waiting for transfers between devices, on_device(): lax.all_to_all(merged, 'expert', split_axis=0, concat_axis=0, tiled=True,...  10.1 us
    pallas_call x1, Pallas kernels, figures(): pl.pallas_call(figures_kernel, grid=(rows // STEP,), in_specs=[pl.BlockSp...  8.17 us
    pallas_call x1, Pallas kernels, merge(): pl.pallas_call(merge_kernel, in_specs=[pl.BlockSpec(memory_space=pl.ANY)]...  6.59 us
    pallas_call x1, Pallas kernels, place(): pl.pallas_call(place_kernel, in_specs=[pl.BlockSpec(memory_space=pltpu.SM...  1.48 us
    pallas_call x1, Pallas kernels, totals(): pl.pallas_call(totals_kernel, in_specs=[pl.BlockSpec(memory_space=pltpu.V...  1.45 us
    unnamed x1, other arithmetic  1.37 us
  transfers between devices with their start and end apart: 1, of which 1 were waited for; matrix products, arithmetic and copies ran while one was open for 8% of the time, Pallas kernels for 16%

profile of v7, /device:TPU:2, one launch (start us, length us, event | category | flops | bytes accessed | tf_op | source)
XLA Modules:
  0.0 61.8 jit_solution(4537642507441907592)
XLA Ops:
  0.6 6.6 %shard_map.76.merged_ref = bf16[32,32,896]{2,1,0:T(8,128)(2,1)} custom-call(s32[3,1,8,112]{3,2,1,0:T(8,128)} %bitcast.4, bf16[1,896,1024]{2,1,0:T(8,128)(2,1)} %base_hbm.1, bf16[3,1,896,1024]{3,2,1,0:T(8,128)(2,1)} %delta_ref.1), custom_call_target="tpu_custom_call" | custom-call | tf_op jit(solution)/shard_map/pallas_call | solution.py:126
  7.2 13.0 %all-to-all-start = ((bf16[32,32,896]{2,1,0:T(8,128)(2,1)}), bf16[32,32,896]{2,1,0:T(8,128)(2,1)S(1)}, u32[]{:S(2)}, u32[]{:S(2)}) async-start(bf16[32,32,896]{2,1,0:T(8,128)(2,1)} %shard_map.76.merged_ref), calls=%async_computation | async-start | bytes 3670016 | tf_op jit(solution)/shard_map/all_to_all | solution.py:236
  20.2 0.0 copy-start
  20.2 8.2 %shard_map.77 = (f32[8,128]{1,0:T(8,128)}, f32[8,128]{1,0:T(8,128)}) custom-call(s32[3,1,8,112]{3,2,1,0:T(8,128)} %bitcast.5, bf16[3,1,896,1024]{3,2,1,0:T(8,128)(2,1)} %delta_ref.1, bf16[32,32,896]{2,1,0:T(8,128)(2,1)} %shard_map.76.merged_ref), custom_call_target="tpu_custom_call" | custom-call | tf_op jit(solution)/shard_map/pallas_call | solution.py:172
  28.4 0.0 copy-done
  28.4 0.6 dynamic-slice
  29.6 1.3 %reduce_max.9 = f32[]{:T(128)} reduce(f32[8,128]{1,0:T(8,128)} %get-tuple-element.9, f32[]{:T(128)} %constant.2.clone.1), dimensions={0,1}, to_apply=%region_1.0 | reduce | flops 1023 | bytes 4104 | tf_op jit(solution)/shard_map/reduce_max | solution.py:240
  30.9 1.3 %reduce_sum.9 = f32[]{:T(128)} reduce(f32[8,128]{1,0:T(8,128)} %get-tuple-element.8, f32[]{:T(128)} %constant.1.clone.1), dimensions={0,1}, to_apply=%region_0.0 | reduce | flops 1023 | bytes 4104 | tf_op jit(solution)/shard_map/reduce_sum | solution.py:240
  32.2 1.4 %maximum_dynamic-update-slice_fusion = f32[16]{0:T(128)S(1)} fusion(f32[16]{0:T(128)S(1)} %broadcast, u32[]{:T(128)} %bitcast.3, f32[1]{0:T(128)} %bitcast.2, f32[1]{0:T(128)} %bitcast.1), kind=kLoop, calls=%fused_computation | loop fusion | flops 2 | bytes 76
  33.6 14.6 %all-reduce = f32[16]{0:T(128)S(1)} all-reduce(f32[16]{0:T(128)S(1)} %maximum_dynamic-update-slice_fusion), channel_id=2, replica_groups=mesh['expert'=32,'mp'=8] {'mp'}, use_global_device_ids=true, to_apply=%add | all-reduce | flops 16 | bytes 128
  48.1 0.7 %reshape.6.both_ref = f32[8,2]{1,0:T(8,128)} reshape(f32[16]{0:T(128)S(1)} %all-reduce) | data formatting | bytes 128 | tf_op jit(solution)/shard_map/all_gather | solution.py:241
  48.8 1.4 %shard_map.78 = (f32[1]{0:T(128)}, f32[1]{0:T(128)}, s32[32]{0:T(128)S(4)}) custom-call(f32[8,2]{1,0:T(8,128)} %reshape.6.both_ref, s32[32]{0:T(128)} %order_ref.1, s32[32]{0:T(128)} %constant.6.clone.place_ref), custom_call_target="tpu_custom_call" | custom-call | tf_op jit(solution)/shard_map/pallas_call | solution.py:196
  50.3 10.1 %all-to-all-done.in_ref = bf16[32,32,896]{2,1,0:T(8,128)(2,1)S(1)} async-done(((bf16[32,32,896]{2,1,0:T(8,128)(2,1)}), bf16[32,32,896]{2,1,0:T(8,128)(2,1)S(1)}, u32[]{:S(2)}, u32[]{:S(2)}) %all-to-all-start) | async-done | bytes 1835040 | tf_op jit(solution)/shard_map/all_to_all | solution.py:236
  60.3 1.5 %shard_map.79 = bf16[32,32,896]{2,1,0:T(8,128)(2,1)} custom-call(s32[32]{0:T(128)S(4)} %get-tuple-element.10.source_ref, bf16[32,32,896]{2,1,0:T(8,128)(2,1)S(1)} %all-to-all-done.in_ref), custom_call_target="tpu_custom_call" | custom-call | tf_op jit(solution)/shard_map/pallas_call | solution.py:220
  (1 shorter events, 0.0 us)
Async XLA Ops:
  7.2 53.1 %all-to-all-start = ((bf16[32,32,896]{2,1,0:T(8,128)(2,1)}), bf16[32,32,896]{2,1,0:T(8,128)(2,1)S(1)}, u32[]{:S(2)}, u32[]{:S(2)}) async-start(bf16[32,32,896]{2,1,0:T(8,128)(2,1)} %shard_map.76.merged_ref), calls=%async_computation | async-start | bytes 3670016 | tf_op jit(solution)/shard_map/all_to_all | solution.py:236
  20.2 8.2 %copy-start = (u32[256]{0:T(256)S(1)}, u32[256]{0:T(256)}, u32[]{:S(2)}) copy-start(u32[256]{0:T(256)} %constant.12) | copy-start | bytes 3076
